TPU v7x, 32 devices: a whole 2x2x4 slice. The times are simulated.
32 devices in a mesh: group: 2 (over y), col: 16 (over z, x, core).
Axes of the slice: x: 2, y: 2, z: 4, core: 2. Of those that a mesh axis runs over, the one named last changes fastest.
Arguments:
- estimate: float32 [512, 4096], P('group', 'col'), parts along dimension 0, may hold values from 0.2 to 2.4, as said below
- observed: float32 [512, 4096], P('group', 'col'), parts along dimension 0, may hold values from 0 to 4
- background: float32 [512, 4096], P('group', 'col'), parts along dimension 0, may hold values from 0.5 to 1.5
- sensitivity: float32 [512, 4096], P('group', 'col'), parts along dimension 0, may hold values from 0.5 to 2
- weights: float32 [8, 512, 4096], P(None, 'group', 'col'), parts along dimension 1, may hold values from 0.05 to 0.3
- kernels: float32 [8, 129, 129], replicated, as said below
- valid_mask: int32 [512, 4096], P('group', 'col'), parts along dimension 0, may hold values 0 or 1
- counts: int32 [512, 4096], P('group', 'col'), parts along dimension 0, may hold values from 1 to 8
Outputs:
- updated: float32 [512, 4096], P('group', 'col'), parts along dimension 0
There are 2 independent parts, one for each index of `group`. A program takes and returns all parts, laid end to end along the dimension named above; an argument that names none is the same for every part. Nothing has to cross between parts.
Inputs may be any that keep to these rules, and one draw needn't show every extreme that they name: `kernels`: kernel entries are nonnegative. The estimate is positive.
All inputs are finite; a program needn't handle non-finite values. No bound on the sum of `valid_mask` on one device may be relied on, other than what follows from the above.
Results may differ from a plain program's by a relative error of at most 0.0001.
Values sent between devices are 32-bit elements; how exact they have to be, the bound alone decides.
No kernel may reach another device: no remote copies, remote signals or barrier semaphores. Data moves between devices by JAX's collectives and lax.ppermute only.
A program may use at most 128 MiB of HBM per device.

v0:
```python
import functools

import jax
import jax.numpy as jnp
import numpy as np
from jax import lax
from jax.experimental import pallas as pl
from jax.experimental.pallas import tpu as pltpu
from jax.sharding import PartitionSpec as P

COVER = 8
LANES = 128
VMEM_MIB = 32
BF16 = jnp.bfloat16
F32 = jnp.float32


def halves(table):
    table = table.astype(np.float32)
    high = table.astype(jnp.bfloat16)
    return high, (table - high.astype(np.float32)).astype(jnp.bfloat16)


def waves(length, places):
    angles = 2.0 * np.pi * (np.arange(length // 2) + 0.5)[:, None] * np.asarray(places)[None, :] / length
    return np.concatenate([np.cos(angles), np.sin(angles)], axis=0)


def left_table(table):
    high, low = halves(table)
    return jnp.asarray(np.concatenate([high, low, high], axis=1))


def right_table(table):
    high, low = halves(table)
    return jnp.asarray(np.concatenate([high, high, low], axis=0))


def wide_table(table):
    return jnp.asarray(np.concatenate(halves(table), axis=1))


def split(values):
    high = values.astype(BF16)
    return high, (values - high.astype(F32)).astype(BF16)


def dot(a, b):
    return jnp.dot(a, b, preferred_element_type=F32)


def left_product(table, values):
    high, low = split(values)
    return dot(table[...], jnp.concatenate([high, high, low], axis=0))


def right_product(values, table):
    high, low = split(values)
    return dot(jnp.concatenate([high, low, high], axis=1), table[...])


def to_complex(plane):
    half = plane.shape[0] // 2
    cc, cs = plane[:half, :LANES], plane[:half, LANES:]
    sc, ss = plane[half:, :LANES], plane[half:, LANES:]
    return cc - ss, cs + sc, cc + ss, cs - sc


def from_complex(a, b, c, d):
    top = jnp.concatenate([a + c, b + d], axis=1)
    low = jnp.concatenate([b - d, c - a], axis=1)
    return jnp.concatenate([top, low], axis=0)


def store_spectrum(ref, index, parts):
    half = parts[0].shape[0]
    ref[index, :half, :LANES], ref[index, :half, LANES:] = parts[0], parts[1]
    ref[index, half:, :LANES], ref[index, half:, LANES:] = parts[2], parts[3]


def load_spectrum(ref, index):
    half = ref.shape[1] // 2
    return (
        ref[index, :half, :LANES], ref[index, :half, LANES:],
        ref[index, half:, :LANES], ref[index, half:, LANES:],
    )


def swap(values):
    return pltpu.roll(values, LANES // 2, 1)


def side_of(outer):
    core = lax.axis_index("col") % 2
    return core if outer else 1 - core


def side_columns(ref, side):
    return ref[:, pl.ds(pl.multiple_of(side * LANES, LANES), LANES)]


def numerator(obs, valid, counts):
    return valid.astype(F32) * counts.astype(F32) * (1.0 / COVER) * obs


def blur_pair(est_half, weight_of, spectrum_of, row_f, col_f):
    pair = jnp.concatenate([weight_of(i) * est_half for i in range(2)], axis=1)
    rows = left_product(row_f, pair)
    sums = None
    for i in range(2):
        fa, fb, fc, fd = to_complex(right_product(rows[:, i * LANES:(i + 1) * LANES], col_f))
        ha, hb, hc, hd = spectrum_of(i)
        terms = (fa * ha - fb * hb, fa * hb + fb * ha, fc * hc - fd * hd, fc * hd + fd * hc)
        sums = terms if sums is None else tuple(s + t for s, t in zip(sums, terms))
    return sums


def accumulate(ref, first, sums):
    if not first:
        sums = tuple(s + t for s, t in zip(load_spectrum(ref, 0), sums))
    store_spectrum(ref, 0, sums)


def blur_end(side, obs, bg, valid, counts, row_i, col_i, total, edge, packed, middle, window):
    plane = right_product(from_complex(*load_spectrum(total, 0)), col_i)
    window[...] = left_product(row_i, plane)
    edge[...] = side_columns(window, side)
    middle[...] = side_columns(window, 1 - side)
    num = numerator(obs, valid, counts)
    lane = lax.broadcasted_iota(jnp.int32, (1, LANES), 1)
    num = jnp.where(side == 0, num, swap(num))
    back = jnp.where(side == 0, swap(bg), bg)
    packed[...] = jnp.where(lane < LANES // 2, num, back)


def outer_blur(components, *refs):
    inputs, refs = refs[:13], refs[13:]
    (spectrum, edge, middle), refs = refs[:3], refs[3:]
    held, (cos_columns, sin_columns, total, window, done) = refs[:13], refs[13:]
    columns = (cos_columns, sin_columns)
    side = side_of(True)
    half = pl.ds(pl.multiple_of(side * LANES, LANES), LANES)
    copies = []
    for i, (ref, kept) in enumerate(zip(inputs, held)):
        if i >= 7:
            ref = ref.at[:, :, half] if len(ref.shape) == 3 else ref.at[:, half]
        copies.append(pltpu.make_async_copy(ref, kept, done.at[i]))
    for copy in copies:
        copy.start()
    kernels, col_h, row_h, row_f, col_f, col_i, row_i, est, weights, obs, bg, valid, counts = held
    size = kernels.shape[0]
    padded = row_h.shape[1] // 3
    copies[0].wait()
    copies[1].wait()
    flat = kernels[...].reshape(size * components, size)
    plane = right_product(flat, col_h)
    for part, ref in enumerate(columns):
        ref[:size * components] = plane[:, part * LANES:(part + 1) * LANES]
        ref[size * components:] = jnp.zeros(((padded - size) * components, LANES), F32)
    for i in (2, 3, 4, 7, 8):
        copies[i].wait()

    def spectrum_of(k):
        places = pl.ds(k, padded, stride=components)
        rows = jnp.concatenate([ref[places, :] for ref in columns], axis=1)
        parts = to_complex(left_product(row_h, rows))
        store_spectrum(spectrum, k, parts)
        return parts

    for k in range(0, components, 2):
        sums = blur_pair(
            est[...], lambda i: weights[k + i], lambda i: spectrum_of(k + i), row_f, col_f
        )
        accumulate(total, k == 0, sums)
    for i in (5, 6, 9, 10, 11, 12):
        copies[i].wait()
    blur_end(
        side, obs[...], bg[...], valid[...], counts[...], row_i, col_i, total,
        edge.at[:, :LANES], edge.at[:, LANES:], middle, window,
    )


def inner_blur(
    est, obs, bg, valid, counts, weights, spectrum, row_f, col_f, row_i, col_i,
    edge, packed, middle, total, window,
):
    side = side_of(False)
    for k in range(0, weights.shape[0], 2):
        sums = blur_pair(
            side_columns(est, side), lambda i: side_columns(weights.at[k + i], side),
            lambda i: load_spectrum(spectrum, k + i), row_f, col_f,
        )
        accumulate(total, k == 0, sums)
    tiles = (side_columns(ref, side) for ref in (obs, bg, valid, counts))
    blur_end(side, *tiles, row_i, col_i, total, edge, packed, middle, window)


def correct_half(
    outer, est, obs, bg, sens, valid, counts, weights, spectrum, edge, received, packed, middle, other,
    row_f, col_w, row_i, col_i, updated, ratio, held, total, done=None,
):
    side = side_of(outer)
    lane = lax.broadcasted_iota(jnp.int32, (1, LANES), 1)
    left = lane < LANES // 2
    num = numerator(obs[...], valid[...], counts[...])

    def centre(own):
        return jnp.where(left, swap(own[:, :LANES]), swap(own[:, LANES:]))

    def at_edge(own):
        return swap(jnp.where(side == 0, own[:, :LANES], own[:, LANES:]))

    def divided(num, blurred, back):
        return jnp.where(num > 0.0, num / (blurred + back), 0.0)

    packed = packed[...]
    turned = swap(packed)
    from_other = (lane >= LANES // 2) == (side == 1)
    edge_num = jnp.where(from_other, jnp.where(side == 0, packed, turned), at_edge(num))
    edge_back = jnp.where(from_other, jnp.where(side == 0, turned, packed), at_edge(bg[...]))
    first = pl.ds(pl.multiple_of(side * LANES, LANES), LANES)
    second = pl.ds(pl.multiple_of((1 - side) * LANES, LANES), LANES)
    ratio[:, first] = divided(edge_num, edge[...] + received[...], edge_back)
    ratio[:, second] = divided(centre(num), middle[...] + other[...], centre(bg[...]))
    store_spectrum(held, 0, to_complex(right_product(left_product(row_f, ratio[...]), col_w)))

    for k in range(0, weights.shape[0], 2):
        planes = []
        a, b, c, d = load_spectrum(held, 0)
        for i in range(2):
            ha, hb, hc, hd = load_spectrum(spectrum, k + i)
            plane = from_complex(a * ha + b * hb, b * ha - a * hb, c * hc + d * hd, d * hc - c * hd)
            high, low = split(plane)
            both = dot(high, col_i[...])
            planes.append(both[:, :LANES] + (both[:, LANES:] + dot(low, col_i[:, :LANES])))
        pair = left_product(row_i, jnp.concatenate(planes, axis=1))
        sums = (
            side_columns(weights.at[k], side) * pair[:, :LANES]
            + side_columns(weights.at[k + 1], side) * pair[:, LANES:]
        )
        total[...] = sums if k == 0 else total[...] + sums

    result = side_columns(est, side) * total[...] / side_columns(sens, side)
    if done is None:
        updated[...] = result
    else:
        updated[:, first] = result
        updated[:, second] = done[...]


def inner_correct(*refs):
    correct_half(False, *refs)


def outer_correct(*refs):
    edge, received, middle, other, done = refs[8:13]
    correct_half(
        True, *refs[:8], edge.at[:, :LANES], received.at[:, :LANES], received.at[:, LANES:],
        middle, other, *refs[13:], done=done,
    )


def call(kernel, name, flops, args, outs, scratch, space=pltpu.VMEM):
    size = sum(a.size * a.dtype.itemsize for a in args)
    if space is pltpu.HBM:
        args = [pltpu.with_memory_space_constraint(a, pltpu.HBM) for a in args]
    return pl.pallas_call(
        kernel,
        in_specs=[pl.BlockSpec(memory_space=space)] * len(args),
        out_specs=[pl.BlockSpec(memory_space=pltpu.VMEM)] * len(outs),
        out_shape=outs,
        scratch_shapes=scratch,
        compiler_params=pltpu.CompilerParams(vmem_limit_bytes=VMEM_MIB * 2**20),
        cost_estimate=pl.CostEstimate(flops=flops // 100, bytes_accessed=size // 100, transcendentals=0),
        name=name,
    )(*args)


def local(estimate, observed, background, sensitivity, weights, kernels, valid_mask, counts):
    rows, cols = estimate.shape
    components, size = kernels.shape[0], kernels.shape[-1]
    halo = (size - 1) // 2
    half_cols = cols // 2
    row_len, col_len = rows + halo, half_cols + 2 * halo
    inner_rows, inner_cols = np.arange(rows), np.arange(half_cols)
    wide_cols = np.arange(-halo, half_cols + halo)
    offsets = np.arange(-halo, halo + 1)
    padded = -(-size // 16) * 16
    row_h = np.pad(waves(row_len, offsets), ((0, 0), (0, padded - size)))
    row_f = left_table(waves(row_len, inner_rows))
    row_i = left_table(waves(row_len, inner_rows).T / row_len)
    row_h = left_table(row_h)
    col_h = right_table(waves(col_len, offsets).T)
    col_f = right_table(waves(col_len, inner_cols).T)
    col_w = right_table(waves(col_len, wide_cols).T)
    col_iw = right_table(waves(col_len, wide_cols) * (2.0 / col_len))
    col_i = wide_table(waves(col_len, inner_cols) * (2.0 / col_len))

    count = lax.axis_size("col")
    between = [(i, i + 1) for i in range(1, count - 1, 2)]
    between += [(j, i) for i, j in between]
    within = [(i, i ^ 1) for i in range(count)]

    macs = 3 * components * row_len * half_cols * (rows + 2 * col_len)
    plane = jax.ShapeDtypeStruct((rows, LANES), F32)
    wide = jax.ShapeDtypeStruct((rows, 2 * LANES), F32)
    spectra = jax.ShapeDtypeStruct((components, row_len, col_len), F32)
    total = pltpu.VMEM((1, row_len, col_len), F32)
    window = pltpu.VMEM((rows, col_len), F32)
    tiles = (observed, background, valid_mask, counts)
    tables = (col_h, row_h, row_f, col_f, col_iw, row_i)
    turned = jnp.transpose(kernels, (1, 0, 2))
    held = [pltpu.VMEM(a.shape, a.dtype) for a in (turned, *tables)]
    held += [
        pltpu.VMEM(a.shape[:-1] + (half_cols,), a.dtype) for a in (estimate, weights, *tiles)
    ]
    columns = pltpu.VMEM((padded * components, LANES), F32)
    spectrum, edge_o, middle_o = call(
        functools.partial(outer_blur, components), "outer_blur", 4 * macs,
        (turned, *tables, estimate, weights, *tiles), (spectra, wide, plane),
        [*held, columns, columns, total, window, pltpu.SemaphoreType.DMA((len(held),))],
        pltpu.HBM,
    )
    received_o = lax.ppermute(edge_o, "col", between)
    edge_i, packed_i, middle_i = call(
        inner_blur, "inner_blur", 2 * macs,
        (estimate, *tiles, weights, spectrum, row_f, col_f, row_i, col_iw),
        (plane, plane, plane), [total, window],
    )
    received_i = (lax.ppermute(edge_i, "col", within), lax.ppermute(packed_i, "col", within))
    shared = (
        estimate, observed, background, sensitivity, valid_mask, counts, weights, spectrum
    )
    tables = (row_f, col_w, row_i, col_i)
    scratch = [window, total, pltpu.VMEM((rows, LANES), F32)]
    (half,) = call(
        inner_correct, "inner_correct", 2 * macs,
        (*shared, edge_i, *received_i, middle_i, middle_o, *tables), (plane,), scratch,
    )
    (updated,) = call(
        outer_correct, "outer_correct", 2 * macs,
        (*shared, edge_o, received_o, middle_o, middle_i, half, *tables), (wide,), scratch,
    )
    return updated


def solution(mesh):
    tile = P("group", "col")
    placed = (tile, tile, tile, tile, P(None, "group", "col"), P(), tile, tile)
    return jax.shard_map(local, mesh=mesh, in_specs=placed, out_specs=tile, check_vma=False)
```

profile of v0, /device:TPU:0, one launch (start us, length us, event | category | flops | bytes accessed | tf_op | source)
XLA Modules:
  0.0 22.2 jit_solution(12655337622118545590)
XLA Ops:
  0.0 0.0 copy-start
  0.0 0.0 copy-start.1
  0.0 0.0 copy-start.2
  0.0 0.0 copy-start.3
  0.0 0.0 copy-start.4
  0.0 0.0 copy-start.5
  0.0 0.0 copy-start.6
  0.0 0.0 copy-start.7
  0.0 0.0 copy-start.9
  0.1 0.0 copy-start.11
  0.1 6.1 %outer_blur.1 = (f32[8,320,256]{2,1,0:T(8,128)S(1)}, f32[256,256]{1,0:T(8,128)S(1)}, f32[256,128]{1,0:T(8,128)S(1)}) custom-call(f32[129,8,129]{2,1,0:T(8,128)} %bitcast.1, bf16[387,256]{1,0:T(8,128)(2,1)} %constant.19.clone.refs_1_, bf16[320,432]{1,0:T(8,128)(2,1)} %constant.18.clone.refs_2_, bf16[320,768]{1,0:T(8,128)(2,1)} %constant.16.clone.refs_3_.row_f.refs_13_, ...), custom_call_target="tpu_custom_call" | custom-call | flops 30198988 | bytes 59878 | tf_op jit(solution)/shard_map/outer_blur/pallas_call | solution.py:267
  6.2 0.7 %collective-permute-start = (f32[256,256]{1,0:T(8,128)S(1)}, f32[256,256]{1,0:T(8,128)S(1)}, u32[]{:S(2)}, u32[]{:S(2)}) collective-permute-start(f32[256,256]{1,0:T(8,128)S(1)} %get-tuple-element.12.refs_8_), channel_id=1, source_target_pairs={{1,2},{3,4},{5,6},{7,8},{9,10},{11,12},{13,14},{2,1},{4,3},{6,5},{... | collective-permute-start | bytes 786440 | tf_op jit(solution)/shard_map/ppermute | solution.py:324
  6.9 0.0 copy-done
  6.9 0.0 copy-done.1
  6.9 0.0 copy-done.2
  6.9 0.0 copy-done.3
  6.9 0.0 copy-done.4
  7.0 0.0 copy-done.5
  7.0 0.0 copy-done.6
  7.0 0.0 copy-done.7
  7.0 0.0 copy-done.9
  7.0 0.0 copy-done.11
  7.0 0.0 copy-start.8
  7.0 0.0 copy-start.10
  7.0 0.0 copy-start.12
  7.0 2.9 %inner_blur.1 = (f32[256,128]{1,0:T(8,128)S(1)}, f32[256,128]{1,0:T(8,128)S(1)}, f32[256,128]{1,0:T(8,128)S(1)}) custom-call(f32[256,256]{1,0:T(8,128)S(1)} %copy-done.3, f32[256,256]{1,0:T(8,128)S(1)} %copy-done.4, f32[256,256]{1,0:T(8,128)S(1)} %copy-done.5, s32[256,256]{1,0:T(8,128)S(1)} %copy-done.6, s32[256,256]{1,0:T(8,128)S(1)} %copy-done.7, ...), custom_call_target="tpu_custom_call" | custom-call | flops 15099494 | bytes 76021 | tf_op jit(solution)/shard_map/inner_blur/pallas_call | solution.py:267
  9.9 4.3 %collective-permute-start.1 = (f32[256,128]{1,0:T(8,128)S(1)}, f32[256,128]{1,0:T(8,128)S(1)}, u32[]{:S(2)}, u32[]{:S(2)}) collective-permute-start(f32[256,128]{1,0:T(8,128)S(1)} %get-tuple-element.15.refs_8_), channel_id=1, source_target_pairs={{0,1},{1,0},{2,3},{3,2},{4,5},{5,4},{6,7},{7,6},{8,9},{9,8},{10,11... | collective-permute-start | bytes 393224 | tf_op jit(solution)/shard_map/ppermute | solution.py:330
  14.3 0.1 collective-permute-start.2
  14.3 0.9 %collective-permute-done.1.refs_9_ = f32[256,128]{1,0:T(8,128)S(1)} collective-permute-done((f32[256,128]{1,0:T(8,128)S(1)}, f32[256,128]{1,0:T(8,128)S(1)}, u32[]{:S(2)}, u32[]{:S(2)}) %collective-permute-start.1) | collective-permute-done | bytes 131104 | tf_op jit(solution)/shard_map/ppermute | solution.py:330
  15.2 0.4 %collective-permute-done.2.refs_10_ = f32[256,128]{1,0:T(8,128)S(1)} collective-permute-done((f32[256,128]{1,0:T(8,128)S(1)}, f32[256,128]{1,0:T(8,128)S(1)}, u32[]{:S(2)}, u32[]{:S(2)}) %collective-permute-start.2) | collective-permute-done | bytes 131104 | tf_op jit(solution)/shard_map/ppermute | solution.py:330
  15.6 0.0 copy-done.8
  15.6 0.0 copy-done.10
  15.6 0.0 copy-done.12
  15.6 2.9 %inner_correct.1.refs_12_ = f32[256,128]{1,0:T(8,128)S(1)} custom-call(f32[256,256]{1,0:T(8,128)S(1)} %copy-done.3, f32[256,256]{1,0:T(8,128)S(1)} %copy-done.4, f32[256,256]{1,0:T(8,128)S(1)} %copy-done.5, f32[256,256]{1,0:T(8,128)S(1)} %copy-done.10, s32[256,256]{1,0:T(8,128)S(1)} %copy-done.6, s32[256,256]{1,0:T(8,128)S(1)} %copy-done.7, ...), custom_call_target="tpu_custom_call" | custom-call | flops 15099494 | bytes 84541 | tf_op jit(solution)/shard_map/inner_correct/pallas_call | solution.py:267
  18.6 0.0 collective-permute-done.refs_9_
  18.6 3.6 %outer_correct.1 = f32[256,256]{1,0:T(8,128)} custom-call(f32[256,256]{1,0:T(8,128)S(1)} %copy-done.3, f32[256,256]{1,0:T(8,128)S(1)} %copy-done.4, f32[256,256]{1,0:T(8,128)S(1)} %copy-done.5, f32[256,256]{1,0:T(8,128)S(1)} %copy-done.10, s32[256,256]{1,0:T(8,128)S(1)} %copy-done.6, s32[256,256]{1,0:T(8,128)S(1)} %copy-done.7, f32[8,256,256]{2,1,0:T(8,128)S(1)} %copy-done, ...), custom_call_target="tpu_custom_call" | custom-call | flops 15099494 | bytes 87162 | tf_op jit(solution)/shard_map/outer_correct/pallas_call | solution.py:267
Async XLA Ops:
  0.0 6.9 %copy-start = (f32[8,256,256]{2,1,0:T(8,128)S(1)}, f32[8,256,256]{2,1,0:T(8,128)}, u32[]{:S(2)}) copy-start(f32[8,256,256]{2,1,0:T(8,128)} %refs_6_.4) | copy-start | bytes 6291460
  0.0 6.9 %copy-start.1 = (bf16[256,960]{1,0:T(8,128)(2,1)S(1)}, bf16[256,960]{1,0:T(8,128)(2,1)}, u32[]{:S(2)}) copy-start(bf16[256,960]{1,0:T(8,128)(2,1)} %constant.17.clone.refs_6_.row_i.refs_15_) | copy-start | bytes 1474564
  0.0 6.9 %copy-start.2 = (bf16[320,768]{1,0:T(8,128)(2,1)S(1)}, bf16[320,768]{1,0:T(8,128)(2,1)}, u32[]{:S(2)}) copy-start(bf16[320,768]{1,0:T(8,128)(2,1)} %constant.16.clone.refs_3_.row_f.refs_13_) | copy-start | bytes 1474564
  0.0 6.9 %copy-start.3 = (f32[256,256]{1,0:T(8,128)S(1)}, f32[256,256]{1,0:T(8,128)}, u32[]{:S(2)}) copy-start(f32[256,256]{1,0:T(8,128)} %refs_0_.3) | copy-start | bytes 786436
  0.0 6.9 %copy-start.4 = (f32[256,256]{1,0:T(8,128)S(1)}, f32[256,256]{1,0:T(8,128)}, u32[]{:S(2)}) copy-start(f32[256,256]{1,0:T(8,128)} %refs_1_.4) | copy-start | bytes 786436
  0.0 6.9 %copy-start.5 = (f32[256,256]{1,0:T(8,128)S(1)}, f32[256,256]{1,0:T(8,128)}, u32[]{:S(2)}) copy-start(f32[256,256]{1,0:T(8,128)} %refs_2_.4) | copy-start | bytes 786436
  0.0 6.9 %copy-start.6 = (s32[256,256]{1,0:T(8,128)S(1)}, s32[256,256]{1,0:T(8,128)}, u32[]{:S(2)}) copy-start(s32[256,256]{1,0:T(8,128)} %refs_4_.4) | copy-start | bytes 786436
  0.0 6.9 %copy-start.7 = (s32[256,256]{1,0:T(8,128)S(1)}, s32[256,256]{1,0:T(8,128)}, u32[]{:S(2)}) copy-start(s32[256,256]{1,0:T(8,128)} %refs_5_.4) | copy-start | bytes 786436
  0.0 6.9 %copy-start.9 = (bf16[768,256]{1,0:T(8,128)(2,1)S(1)}, bf16[768,256]{1,0:T(8,128)(2,1)}, u32[]{:S(2)}) copy-start(bf16[768,256]{1,0:T(8,128)(2,1)} %constant.22.clone.refs_5_.col_i) | copy-start | bytes 1179652
  0.1 6.9 %copy-start.11 = (bf16[384,256]{1,0:T(8,128)(2,1)S(1)}, bf16[384,256]{1,0:T(8,128)(2,1)}, u32[]{:S(2)}) copy-start(bf16[384,256]{1,0:T(8,128)(2,1)} %constant.20.clone.refs_4_.col_f) | copy-start | bytes 589828
  6.2 12.3 %collective-permute-start = (f32[256,256]{1,0:T(8,128)S(1)}, f32[256,256]{1,0:T(8,128)S(1)}, u32[]{:S(2)}, u32[]{:S(2)}) collective-permute-start(f32[256,256]{1,0:T(8,128)S(1)} %get-tuple-element.12.refs_8_), channel_id=1, source_target_pairs={{1,2},{3,4},{5,6},{7,8},{9,10},{11,12},{13,14},{2,1},{4,3},{6,5},{... | collective-permute-start | bytes 786440 | tf_op jit(solution)/shard_map/ppermute | solution.py:324
  7.0 8.6 %copy-start.8 = (bf16[768,256]{1,0:T(8,128)(2,1)S(1)}, bf16[768,256]{1,0:T(8,128)(2,1)}, u32[]{:S(2)}) copy-start(bf16[768,256]{1,0:T(8,128)(2,1)} %constant.21.clone.refs_14_) | copy-start | bytes 1179652
  7.0 8.6 %copy-start.10 = (f32[256,256]{1,0:T(8,128)S(1)}, f32[256,256]{1,0:T(8,128)}, u32[]{:S(2)}) copy-start(f32[256,256]{1,0:T(8,128)} %refs_3_.4) | copy-start | bytes 786436
  7.0 8.6 %copy-start.12 = (bf16[256,256]{1,0:T(8,128)(2,1)S(1)}, bf16[256,256]{1,0:T(8,128)(2,1)}, u32[]{:S(2)}) copy-start(bf16[256,256]{1,0:T(8,128)(2,1)} %constant.23.clone.refs_16_) | copy-start | bytes 393220
  9.9 5.3 %collective-permute-start.1 = (f32[256,128]{1,0:T(8,128)S(1)}, f32[256,128]{1,0:T(8,128)S(1)}, u32[]{:S(2)}, u32[]{:S(2)}) collective-permute-start(f32[256,128]{1,0:T(8,128)S(1)} %get-tuple-element.15.refs_8_), channel_id=1, source_target_pairs={{0,1},{1,0},{2,3},{3,2},{4,5},{5,4},{6,7},{7,6},{8,9},{9,8},{10,11... | collective-permute-start | bytes 393224 | tf_op jit(solution)/shard_map/ppermute | solution.py:330
  14.3 1.3 %collective-permute-start.2 = (f32[256,128]{1,0:T(8,128)S(1)}, f32[256,128]{1,0:T(8,128)S(1)}, u32[]{:S(2)}, u32[]{:S(2)}) collective-permute-start(f32[256,128]{1,0:T(8,128)S(1)} %get-tuple-element.16), channel_id=1, source_target_pairs={{0,1},{1,0},{2,3},{3,2},{4,5},{5,4},{6,7},{7,6},{8,9},{9,8},{10,11... | collective-permute-start | bytes 393224 | tf_op jit(solution)/shard_map/ppermute | solution.py:330
where the time goes:
time: 22.3 us; the launch traced here: 22.2 us
  Pallas kernels  15.5 us (70%)
  starting transfers between devices  5.11 us (23%)
  waiting for transfers between devices  1.27 us (6%)
    pallas_call x4, Pallas kernels, call(): pl.pallas_call(kernel, in_specs=[pl.BlockSpec(memory_space=space)] * len(...  15.5 us
    ppermute x1, starting transfers between devices, local(): lax.ppermute(edge_i, 'col', within)  4.35 us
    ppermute x1, waiting for transfers between devices, local(): lax.ppermute(edge_i, 'col', within)  0.91 us
    ppermute x1, starting transfers between devices, local(): received_o = lax.ppermute(edge_o, 'col', between)  0.68 us
  transfers between devices with their start and end apart: 3, of which 2 were waited for; matrix products, arithmetic and copies ran while one was open for 0% of the time, Pallas kernels for 26%

commit v1 on v0

--- a/solution.py
+++ b/solution.py
@@ -26,6 +26,24 @@
     return np.concatenate([np.cos(angles), np.sin(angles)], axis=0)
 
 
+def whole_waves(length, places):
+    freqs = np.arange(length // 2)
+    freqs = np.concatenate([freqs[0::2], freqs[1::2]])
+    angles = 2.0 * np.pi * freqs[:, None] * np.asarray(places)[None, :] / length
+    sin = np.sin(angles)
+    sin[0] = np.cos(np.pi * np.asarray(places))
+    return np.cos(angles), sin
+
+
+def parity_waves(length, places):
+    cos, sin = whole_waves(length, places)
+    quarter = length // 4
+    return (
+        np.concatenate([cos[:quarter], sin[:quarter]]),
+        np.concatenate([cos[quarter:], sin[quarter:]]),
+    )
+
+
 def left_table(table):
     high, low = halves(table)
     return jnp.asarray(np.concatenate([high, low, high], axis=1))
@@ -57,18 +75,44 @@
 def right_product(values, table):
     high, low = split(values)
     return dot(jnp.concatenate([high, low, high], axis=1), table[...])
+
+
+def rows_forward(even, odd, values):
+    half = even.shape[1] // 3
+    quarter = even.shape[0] // 2
+    rest = values.shape[0] - half
+    first, second, alone = values[:rest], values[half:], values[rest:half]
+    e = left_product(even, jnp.concatenate([first + second, alone], axis=0))
+    o = left_product(odd, jnp.concatenate([first - second, alone], axis=0))
+    return jnp.concatenate([e[:quarter], o[:quarter], e[quarter:], o[quarter:]], axis=0)
+
+
+def rows_inverse(even, odd, plane, rows):
+    quarter = plane.shape[0] // 4
+    parts = [plane[i * quarter:(i + 1) * quarter] for i in range(4)]
+    e = left_product(even, jnp.concatenate([parts[0], parts[2]], axis=0))
+    o = left_product(odd, jnp.concatenate([parts[1], parts[3]], axis=0))
+    return jnp.concatenate([e + o, (e - o)[:rows - e.shape[0]]], axis=0)
+
+
+def fix_first(first, values):
+    row = lax.broadcasted_iota(jnp.int32, (8, 1), 0)
+    return jnp.concatenate([jnp.where(row == 0, first, values[:8]), values[8:]], axis=0)
 
 
 def to_complex(plane):
     half = plane.shape[0] // 2
     cc, cs = plane[:half, :LANES], plane[:half, LANES:]
     sc, ss = plane[half:, :LANES], plane[half:, LANES:]
-    return cc - ss, cs + sc, cc + ss, cs - sc
+    return (
+        fix_first(cc[:8], cc - ss), fix_first(cs[:8], cs + sc),
+        fix_first(sc[:8], cc + ss), fix_first(ss[:8], cs - sc),
+    )
 
 
 def from_complex(a, b, c, d):
-    top = jnp.concatenate([a + c, b + d], axis=1)
-    low = jnp.concatenate([b - d, c - a], axis=1)
+    top = jnp.concatenate([fix_first(a[:8], a + c), fix_first(b[:8], b + d)], axis=1)
+    low = jnp.concatenate([fix_first(c[:8], b - d), fix_first(d[:8], c - a)], axis=1)
     return jnp.concatenate([top, low], axis=0)
 
 
@@ -103,9 +147,9 @@
     return valid.astype(F32) * counts.astype(F32) * (1.0 / COVER) * obs
 
 
-def blur_pair(est_half, weight_of, spectrum_of, row_f, col_f):
+def blur_pair(est_half, weight_of, spectrum_of, row_e, row_o, col_f):
     pair = jnp.concatenate([weight_of(i) * est_half for i in range(2)], axis=1)
-    rows = left_product(row_f, pair)
+    rows = rows_forward(row_e, row_o, pair)
     sums = None
     for i in range(2):
         fa, fb, fc, fd = to_complex(right_product(rows[:, i * LANES:(i + 1) * LANES], col_f))
@@ -121,9 +165,9 @@
     store_spectrum(ref, 0, sums)
 
 
-def blur_end(side, obs, bg, valid, counts, row_i, col_i, total, edge, packed, middle, window):
+def blur_end(side, obs, bg, valid, counts, inv_e, inv_o, col_i, total, edge, packed, middle, window):
     plane = right_product(from_complex(*load_spectrum(total, 0)), col_i)
-    window[...] = left_product(row_i, plane)
+    window[...] = rows_inverse(inv_e, inv_o, plane, window.shape[0])
     edge[...] = side_columns(window, side)
     middle[...] = side_columns(window, 1 - side)
     num = numerator(obs, valid, counts)
@@ -134,70 +178,90 @@
 
 
 def outer_blur(components, *refs):
-    inputs, refs = refs[:13], refs[13:]
+    inputs, refs = refs[:16], refs[16:]
     (spectrum, edge, middle), refs = refs[:3], refs[3:]
-    held, (cos_columns, sin_columns, total, window, done) = refs[:13], refs[13:]
+    kept, refs = refs[:12], refs[12:]
+    kernels, col_h, row_c, row_s, cos_columns, sin_columns, total, window, done = refs
     columns = (cos_columns, sin_columns)
     side = side_of(True)
-    half = pl.ds(pl.multiple_of(side * LANES, LANES), LANES)
+    near = pl.ds(pl.multiple_of(side * LANES, LANES), LANES)
+    far = pl.ds(pl.multiple_of((1 - side) * LANES, LANES), LANES)
+    held = (kernels, col_h, row_c, row_s, *kept)
     copies = []
-    for i, (ref, kept) in enumerate(zip(inputs, held)):
-        if i >= 7:
-            ref = ref.at[:, :, half] if len(ref.shape) == 3 else ref.at[:, half]
-        copies.append(pltpu.make_async_copy(ref, kept, done.at[i]))
-    for copy in copies:
+    for i, (ref, own) in enumerate(zip(inputs, held)):
+        if i == 8:
+            copies.append((ref.at[:, :, near], own.at[:, :, near]))
+        else:
+            copies.append((ref, own))
+    copies.append((inputs[8].at[:, :, far], held[8].at[:, :, far]))
+    copies = [pltpu.make_async_copy(a, b, done.at[i]) for i, (a, b) in enumerate(copies)]
+    for copy in copies[:9]:
         copy.start()
-    kernels, col_h, row_h, row_f, col_f, col_i, row_i, est, weights, obs, bg, valid, counts = held
+    row_e, row_o, col_f, est, weights, col_i, inv_e, inv_o, obs, bg, valid, counts = kept
     size = kernels.shape[0]
-    padded = row_h.shape[1] // 3
+    centre = size // 2
+    evens, odds = row_c.shape[1] // 3, row_s.shape[1] // 3
+    half = row_s.shape[0]
     copies[0].wait()
     copies[1].wait()
-    flat = kernels[...].reshape(size * components, size)
-    plane = right_product(flat, col_h)
+    above, below = kernels[centre + 1:], [kernels[i:i + 1] for i in range(centre - 1, -1, -1)]
+    below = jnp.concatenate(below, axis=0)
+    folded = jnp.concatenate([above - below, kernels[centre:centre + 1], above + below], axis=0)
+    plane = right_product(folded.reshape(size * components, size), col_h)
+    empty = (odds + evens - size) * components
     for part, ref in enumerate(columns):
         ref[:size * components] = plane[:, part * LANES:(part + 1) * LANES]
-        ref[size * components:] = jnp.zeros(((padded - size) * components, LANES), F32)
-    for i in (2, 3, 4, 7, 8):
-        copies[i].wait()
+        ref[size * components:] = jnp.zeros((empty, LANES), F32)
+    for copy in copies[2:9]:
+        copy.wait()
+    for copy in copies[9:]:
+        copy.start()
 
     def spectrum_of(k):
-        places = pl.ds(k, padded, stride=components)
-        rows = jnp.concatenate([ref[places, :] for ref in columns], axis=1)
-        parts = to_complex(left_product(row_h, rows))
+        def taken(start, count):
+            places = pl.ds(k + start * components, count, stride=components)
+            return jnp.concatenate([ref[places, :] for ref in columns], axis=1)
+
+        cos = left_product(row_c, taken(odds, evens))
+        sin = left_product(row_s, taken(0, odds))
+        sin = fix_first(cos[half:half + 1], sin)
+        parts = to_complex(jnp.concatenate([cos[:half], sin], axis=0))
         store_spectrum(spectrum, k, parts)
         return parts
 
     for k in range(0, components, 2):
         sums = blur_pair(
-            est[...], lambda i: weights[k + i], lambda i: spectrum_of(k + i), row_f, col_f
+            side_columns(est, side), lambda i: side_columns(weights.at[k + i], side),
+            lambda i: spectrum_of(k + i), row_e, row_o, col_f,
         )
         accumulate(total, k == 0, sums)
-    for i in (5, 6, 9, 10, 11, 12):
-        copies[i].wait()
+    for copy in copies[9:]:
+        copy.wait()
+    tiles = (side_columns(ref, side) for ref in (obs, bg, valid, counts))
     blur_end(
-        side, obs[...], bg[...], valid[...], counts[...], row_i, col_i, total,
+        side, *tiles, inv_e, inv_o, col_i, total,
         edge.at[:, :LANES], edge.at[:, LANES:], middle, window,
     )
 
 
 def inner_blur(
-    est, obs, bg, valid, counts, weights, spectrum, row_f, col_f, row_i, col_i,
+    est, obs, bg, valid, counts, weights, spectrum, row_e, row_o, col_f, inv_e, inv_o, col_i,
     edge, packed, middle, total, window,
 ):
     side = side_of(False)
     for k in range(0, weights.shape[0], 2):
         sums = blur_pair(
             side_columns(est, side), lambda i: side_columns(weights.at[k + i], side),
-            lambda i: load_spectrum(spectrum, k + i), row_f, col_f,
+            lambda i: load_spectrum(spectrum, k + i), row_e, row_o, col_f,
         )
         accumulate(total, k == 0, sums)
     tiles = (side_columns(ref, side) for ref in (obs, bg, valid, counts))
-    blur_end(side, *tiles, row_i, col_i, total, edge, packed, middle, window)
+    blur_end(side, *tiles, inv_e, inv_o, col_i, total, edge, packed, middle, window)
 
 
 def correct_half(
     outer, est, obs, bg, sens, valid, counts, weights, spectrum, edge, received, packed, middle, other,
-    row_f, col_w, row_i, col_i, updated, ratio, held, total, done=None,
+    row_e, row_o, col_w, inv_e, inv_o, col_i, updated, ratio, held, total, done=None,
 ):
     side = side_of(outer)
     lane = lax.broadcasted_iota(jnp.int32, (1, LANES), 1)
@@ -222,7 +286,7 @@
     second = pl.ds(pl.multiple_of((1 - side) * LANES, LANES), LANES)
     ratio[:, first] = divided(edge_num, edge[...] + received[...], edge_back)
     ratio[:, second] = divided(centre(num), middle[...] + other[...], centre(bg[...]))
-    store_spectrum(held, 0, to_complex(right_product(left_product(row_f, ratio[...]), col_w)))
+    store_spectrum(held, 0, to_complex(right_product(rows_forward(row_e, row_o, ratio[...]), col_w)))
 
     for k in range(0, weights.shape[0], 2):
         planes = []
@@ -233,7 +297,7 @@
             high, low = split(plane)
             both = dot(high, col_i[...])
             planes.append(both[:, :LANES] + (both[:, LANES:] + dot(low, col_i[:, :LANES])))
-        pair = left_product(row_i, jnp.concatenate(planes, axis=1))
+        pair = rows_inverse(inv_e, inv_o, jnp.concatenate(planes, axis=1), total.shape[0])
         sums = (
             side_columns(weights.at[k], side) * pair[:, :LANES]
             + side_columns(weights.at[k + 1], side) * pair[:, LANES:]
@@ -282,14 +346,18 @@
     halo = (size - 1) // 2
     half_cols = cols // 2
     row_len, col_len = rows + halo, half_cols + 2 * halo
-    inner_rows, inner_cols = np.arange(rows), np.arange(half_cols)
+    inner_cols = np.arange(half_cols)
     wide_cols = np.arange(-halo, half_cols + halo)
     offsets = np.arange(-halo, halo + 1)
-    padded = -(-size // 16) * 16
-    row_h = np.pad(waves(row_len, offsets), ((0, 0), (0, padded - size)))
-    row_f = left_table(waves(row_len, inner_rows))
-    row_i = left_table(waves(row_len, inner_rows).T / row_len)
-    row_h = left_table(row_h)
+    quarter = np.arange(row_len // 2)
+    row_e, row_o = (left_table(t) for t in parity_waves(row_len, quarter))
+    inv_e, inv_o = (left_table(t.T / row_len) for t in parity_waves(row_len, quarter))
+    evens = -(-(halo + 1) // 16) * 16
+    cos, sin = whole_waves(row_len, np.arange(halo + 1))
+    cos = np.concatenate([cos, sin[:1]])
+    row_c = left_table(np.pad(cos, ((0, -len(cos) % 16), (0, evens - halo - 1))))
+    sin[0] = 0.0
+    row_s = left_table(sin[:, 1:])
     col_h = right_table(waves(col_len, offsets).T)
     col_f = right_table(waves(col_len, inner_cols).T)
     col_w = right_table(waves(col_len, wide_cols).T)
@@ -307,31 +375,36 @@
     spectra = jax.ShapeDtypeStruct((components, row_len, col_len), F32)
     total = pltpu.VMEM((1, row_len, col_len), F32)
     window = pltpu.VMEM((rows, col_len), F32)
+    turned = jnp.transpose(kernels, (1, 0, 2))
+    first = (turned, col_h, row_c, row_s)
+    kept = (
+        row_e, row_o, col_f, estimate, weights, col_iw, inv_e, inv_o,
+        observed, background, valid_mask, counts,
+    )
+    columns = pltpu.VMEM(((halo + evens) * components, LANES), F32)
+    spectrum, edge_o, middle_o, *kept = call(
+        functools.partial(outer_blur, components), "outer_blur", 4 * macs, (*first, *kept),
+        (spectra, wide, plane, *(jax.ShapeDtypeStruct(a.shape, a.dtype) for a in kept)),
+        [
+            *(pltpu.VMEM(a.shape, a.dtype) for a in first), columns, columns, total, window,
+            pltpu.SemaphoreType.DMA((len(first) + len(kept) + 1,)),
+        ],
+        pltpu.HBM,
+    )
+    row_e, row_o, col_f, estimate, weights, col_iw, inv_e, inv_o = kept[:8]
+    observed, background, valid_mask, counts = kept[8:]
     tiles = (observed, background, valid_mask, counts)
-    tables = (col_h, row_h, row_f, col_f, col_iw, row_i)
-    turned = jnp.transpose(kernels, (1, 0, 2))
-    held = [pltpu.VMEM(a.shape, a.dtype) for a in (turned, *tables)]
-    held += [
-        pltpu.VMEM(a.shape[:-1] + (half_cols,), a.dtype) for a in (estimate, weights, *tiles)
-    ]
-    columns = pltpu.VMEM((padded * components, LANES), F32)
-    spectrum, edge_o, middle_o = call(
-        functools.partial(outer_blur, components), "outer_blur", 4 * macs,
-        (turned, *tables, estimate, weights, *tiles), (spectra, wide, plane),
-        [*held, columns, columns, total, window, pltpu.SemaphoreType.DMA((len(held),))],
-        pltpu.HBM,
-    )
     received_o = lax.ppermute(edge_o, "col", between)
     edge_i, packed_i, middle_i = call(
         inner_blur, "inner_blur", 2 * macs,
-        (estimate, *tiles, weights, spectrum, row_f, col_f, row_i, col_iw),
+        (estimate, *tiles, weights, spectrum, row_e, row_o, col_f, inv_e, inv_o, col_iw),
         (plane, plane, plane), [total, window],
     )
     received_i = (lax.ppermute(edge_i, "col", within), lax.ppermute(packed_i, "col", within))
     shared = (
         estimate, observed, background, sensitivity, valid_mask, counts, weights, spectrum
     )
-    tables = (row_f, col_w, row_i, col_i)
+    tables = (row_e, row_o, col_w, inv_e, inv_o, col_i)
     scratch = [window, total, pltpu.VMEM((rows, LANES), F32)]
     (half,) = call(
         inner_correct, "inner_correct", 2 * macs,

time: 22.3 us -> 20.7 us (0.928)
  Pallas kernels: 15.5 us -> 14.1 us
    ppermute x1, starting transfers between devices: 4.35 us -> 0.08 us  [local(): lax.ppermute(edge_i, 'col', within)]
    ppermute x1, starting transfers between devices: 0.08 us -> 4.33 us  [local(): lax.ppermute(packed_i, 'col', within)]
    pallas_call x4, Pallas kernels: 15.5 us -> 14.1 us  [call(): pl.pallas_call(kernel, in_specs=[pl.BlockSpec(memory_space=space)] * len(...]
    ppermute x1, waiting for transfers between devices: 0.91 us -> 0.36 us  [local(): lax.ppermute(edge_i, 'col', within)]
    ppermute x1, waiting for transfers between devices: 0.36 us -> 0.91 us  [local(): lax.ppermute(packed_i, 'col', within)]
where the time goes in v1:
time: 20.7 us; the launch traced here: 20.6 us
  Pallas kernels  14.1 us (68%)
  starting transfers between devices  5.08 us (25%)
  waiting for transfers between devices  1.27 us (6%)
    pallas_call x4, Pallas kernels, call(): pl.pallas_call(kernel, in_specs=[pl.BlockSpec(memory_space=space)] * len(...  14.1 us
    ppermute x1, starting transfers between devices, local(): lax.ppermute(packed_i, 'col', within)  4.33 us
    ppermute x1, waiting for transfers between devices, local(): lax.ppermute(packed_i, 'col', within)  0.91 us
    ppermute x1, starting transfers between devices, local(): received_o = lax.ppermute(edge_o, 'col', between)  0.68 us
  transfers between devices with their start and end apart: 3, of which 2 were waited for; matrix products, arithmetic and copies ran while one was open for 0% of the time, Pallas kernels for 26%

profile of v1, /device:TPU:0, one launch (start us, length us, event | category | flops | bytes accessed | tf_op | source)
XLA Modules:
  0.0 20.6 jit_solution(16046555085407189487)
XLA Ops:
  0.0 5.2 %outer_blur.1 = (f32[8,320,256]{2,1,0:T(8,128)S(1)}, f32[256,256]{1,0:T(8,128)S(1)}, f32[256,128]{1,0:T(8,128)S(1)}, bf16[160,480]{1,0:T(8,128)(2,1)S(1)}, bf16[...) custom-call(f32[129,8,129]{2,1,0:T(8,128)} %bitcast.1, ...), custom_call_target="tpu_custom_call" | custom-call | flops 30198988 | bytes 54886 | tf_op jit(solution)/shard_map/outer_blur/pallas_call | solution.py:331
  5.2 0.7 %collective-permute-start = (f32[256,256]{1,0:T(8,128)S(1)}, f32[256,256]{1,0:T(8,128)S(1)}, u32[]{:S(2)}, u32[]{:S(2)}) collective-permute-start(f32[256,256]{1,0:T(8,128)S(1)} %get-tuple-element.30.refs_8_), channel_id=1, source_target_pairs={{1,2},{3,4},{5,6},{7,8},{9,10},{11,12},{13,14},{2,1},{4,3},{6,5},{... | collective-permute-start | bytes 786440 | tf_op jit(solution)/shard_map/ppermute | solution.py:397
  5.9 0.0 copy-start
  5.9 0.0 copy-start.1
  5.9 0.0 copy-start.2
  5.9 2.5 %inner_blur.1 = (f32[256,128]{1,0:T(8,128)S(1)}, f32[256,128]{1,0:T(8,128)S(1)}, f32[256,128]{1,0:T(8,128)S(1)}) custom-call(f32[256,256]{1,0:T(8,128)S(1)} %get-tuple-element.23.est.refs_0_, f32[256,256]{1,0:T(8,128)S(1)} %get-tuple-element.24.obs.refs_1_, f32[256,256]{1,0:T(8,128)S(1)} %get-tuple-element.25.bg.refs_2_, ...), custom_call_target="tpu_custom_call" | custom-call | flops 15099494 | bytes 72335 | tf_op jit(solution)/shard_map/inner_blur/pallas_call | solution.py:331
  8.4 4.3 %collective-permute-start.2 = (f32[256,128]{1,0:T(8,128)S(1)}, f32[256,128]{1,0:T(8,128)S(1)}, u32[]{:S(2)}, u32[]{:S(2)}) collective-permute-start(f32[256,128]{1,0:T(8,128)S(1)} %get-tuple-element.40), channel_id=1, source_target_pairs={{0,1},{1,0},{2,3},{3,2},{4,5},{5,4},{6,7},{7,6},{8,9},{9,8},{10,11... | collective-permute-start | bytes 393224 | tf_op jit(solution)/shard_map/ppermute | solution.py:403
  12.8 0.1 collective-permute-start.1
  12.8 0.9 %collective-permute-done.2.refs_10_ = f32[256,128]{1,0:T(8,128)S(1)} collective-permute-done((f32[256,128]{1,0:T(8,128)S(1)}, f32[256,128]{1,0:T(8,128)S(1)}, u32[]{:S(2)}, u32[]{:S(2)}) %collective-permute-start.2) | collective-permute-done | bytes 131104 | tf_op jit(solution)/shard_map/ppermute | solution.py:403
  13.7 0.4 %collective-permute-done.1.refs_9_ = f32[256,128]{1,0:T(8,128)S(1)} collective-permute-done((f32[256,128]{1,0:T(8,128)S(1)}, f32[256,128]{1,0:T(8,128)S(1)}, u32[]{:S(2)}, u32[]{:S(2)}) %collective-permute-start.1) | collective-permute-done | bytes 131104 | tf_op jit(solution)/shard_map/ppermute | solution.py:403
  14.1 0.0 copy-done
  14.1 0.0 copy-done.1
  14.1 0.0 copy-done.2
  14.1 2.9 %inner_correct.1.refs_12_ = f32[256,128]{1,0:T(8,128)S(1)} custom-call(f32[256,256]{1,0:T(8,128)S(1)} %get-tuple-element.23.est.refs_0_, f32[256,256]{1,0:T(8,128)S(1)} %get-tuple-element.24.obs.refs_1_, f32[256,256]{1,0:T(8,128)S(1)} %get-tuple-element.25.bg.refs_2_, f32[256,256]{1,0:T(8,128)S(1)} %copy-done.1, ...), custom_call_target="tpu_custom_call" | custom-call | flops 15099494 | bytes 80855 | tf_op jit(solution)/shard_map/inner_correct/pallas_call | solution.py:331
  17.0 0.0 collective-permute-done.refs_9_
  17.0 3.5 %outer_correct.1 = f32[256,256]{1,0:T(8,128)} custom-call(f32[256,256]{1,0:T(8,128)S(1)} %get-tuple-element.23.est.refs_0_, f32[256,256]{1,0:T(8,128)S(1)} %get-tuple-element.24.obs.refs_1_, f32[256,256]{1,0:T(8,128)S(1)} %get-tuple-element.25.bg.refs_2_, f32[256,256]{1,0:T(8,128)S(1)} %copy-done.1, s32[256,256]{1,0:T(8,128)S(1)} %get-tuple-element.26.valid.refs_4_, ...), custom_call_target="tpu_custom_call" | custom-call | flops 15099494 | bytes 83476 | tf_op jit(solution)/shard_map/outer_correct/pallas_call | solution.py:331
Async XLA Ops:
  5.2 11.8 %collective-permute-start = (f32[256,256]{1,0:T(8,128)S(1)}, f32[256,256]{1,0:T(8,128)S(1)}, u32[]{:S(2)}, u32[]{:S(2)}) collective-permute-start(f32[256,256]{1,0:T(8,128)S(1)} %get-tuple-element.30.refs_8_), channel_id=1, source_target_pairs={{1,2},{3,4},{5,6},{7,8},{9,10},{11,12},{13,14},{2,1},{4,3},{6,5},{... | collective-permute-start | bytes 786440 | tf_op jit(solution)/shard_map/ppermute | solution.py:397
  5.9 8.2 %copy-start = (bf16[768,256]{1,0:T(8,128)(2,1)S(1)}, bf16[768,256]{1,0:T(8,128)(2,1)}, u32[]{:S(2)}) copy-start(bf16[768,256]{1,0:T(8,128)(2,1)} %constant.30.clone.refs_15_) | copy-start | bytes 1179652
  5.9 8.2 %copy-start.1 = (f32[256,256]{1,0:T(8,128)S(1)}, f32[256,256]{1,0:T(8,128)}, u32[]{:S(2)}) copy-start(f32[256,256]{1,0:T(8,128)} %refs_3_.4) | copy-start | bytes 786436
  5.9 8.2 %copy-start.2 = (bf16[256,256]{1,0:T(8,128)(2,1)S(1)}, bf16[256,256]{1,0:T(8,128)(2,1)}, u32[]{:S(2)}) copy-start(bf16[256,256]{1,0:T(8,128)(2,1)} %constant.32.clone.refs_18_) | copy-start | bytes 393220
  8.4 5.3 %collective-permute-start.2 = (f32[256,128]{1,0:T(8,128)S(1)}, f32[256,128]{1,0:T(8,128)S(1)}, u32[]{:S(2)}, u32[]{:S(2)}) collective-permute-start(f32[256,128]{1,0:T(8,128)S(1)} %get-tuple-element.40), channel_id=1, source_target_pairs={{0,1},{1,0},{2,3},{3,2},{4,5},{5,4},{6,7},{7,6},{8,9},{9,8},{10,11... | collective-permute-start | bytes 393224 | tf_op jit(solution)/shard_map/ppermute | solution.py:403
  12.8 1.3 %collective-permute-start.1 = (f32[256,128]{1,0:T(8,128)S(1)}, f32[256,128]{1,0:T(8,128)S(1)}, u32[]{:S(2)}, u32[]{:S(2)}) collective-permute-start(f32[256,128]{1,0:T(8,128)S(1)} %get-tuple-element.39.refs_8_), channel_id=1, source_target_pairs={{0,1},{1,0},{2,3},{3,2},{4,5},{5,4},{6,7},{7,6},{8,9},{9,8},{10,11... | collective-permute-start | bytes 393224 | tf_op jit(solution)/shard_map/ppermute | solution.py:403

commit v2 on v1

--- a/solution.py
+++ b/solution.py
@@ -147,16 +147,24 @@
     return valid.astype(F32) * counts.astype(F32) * (1.0 / COVER) * obs
 
 
-def blur_pair(est_half, weight_of, spectrum_of, row_e, row_o, col_f):
-    pair = jnp.concatenate([weight_of(i) * est_half for i in range(2)], axis=1)
-    rows = rows_forward(row_e, row_o, pair)
-    sums = None
-    for i in range(2):
-        fa, fb, fc, fd = to_complex(right_product(rows[:, i * LANES:(i + 1) * LANES], col_f))
-        ha, hb, hc, hd = spectrum_of(i)
-        terms = (fa * ha - fb * hb, fa * hb + fb * ha, fc * hc - fd * hd, fc * hd + fd * hc)
-        sums = terms if sums is None else tuple(s + t for s, t in zip(sums, terms))
-    return sums
+def blur_pairs(est_half, weight_of, spectrum_of, components, row_e, row_o, col_f, total):
+    def ahead(k):
+        pair = jnp.concatenate([weight_of(k + i) * est_half for i in range(2)], axis=1)
+        rows = rows_forward(row_e, row_o, pair)
+        return rows, [spectrum_of(k + i) for i in range(2)]
+
+    coming = ahead(0)
+    for k in range(0, components, 2):
+        rows, spectra = coming
+        if k + 2 < components:
+            coming = ahead(k + 2)
+        sums = None
+        for i in range(2):
+            fa, fb, fc, fd = to_complex(right_product(rows[:, i * LANES:(i + 1) * LANES], col_f))
+            ha, hb, hc, hd = spectra[i]
+            terms = (fa * ha - fb * hb, fa * hb + fb * ha, fc * hc - fd * hd, fc * hd + fd * hc)
+            sums = terms if sums is None else tuple(s + t for s, t in zip(sums, terms))
+        accumulate(total, k == 0, sums)
 
 
 def accumulate(ref, first, sums):
@@ -229,12 +237,10 @@
         store_spectrum(spectrum, k, parts)
         return parts
 
-    for k in range(0, components, 2):
-        sums = blur_pair(
-            side_columns(est, side), lambda i: side_columns(weights.at[k + i], side),
-            lambda i: spectrum_of(k + i), row_e, row_o, col_f,
-        )
-        accumulate(total, k == 0, sums)
+    blur_pairs(
+        side_columns(est, side), lambda k: side_columns(weights.at[k], side), spectrum_of,
+        components, row_e, row_o, col_f, total,
+    )
     for copy in copies[9:]:
         copy.wait()
     tiles = (side_columns(ref, side) for ref in (obs, bg, valid, counts))
@@ -249,12 +255,10 @@
     edge, packed, middle, total, window,
 ):
     side = side_of(False)
-    for k in range(0, weights.shape[0], 2):
-        sums = blur_pair(
-            side_columns(est, side), lambda i: side_columns(weights.at[k + i], side),
-            lambda i: load_spectrum(spectrum, k + i), row_e, row_o, col_f,
-        )
-        accumulate(total, k == 0, sums)
+    blur_pairs(
+        side_columns(est, side), lambda k: side_columns(weights.at[k], side),
+        lambda k: load_spectrum(spectrum, k), weights.shape[0], row_e, row_o, col_f, total,
+    )
     tiles = (side_columns(ref, side) for ref in (obs, bg, valid, counts))
     blur_end(side, *tiles, inv_e, inv_o, col_i, total, edge, packed, middle, window)
 
@@ -288,7 +292,7 @@
     ratio[:, second] = divided(centre(num), middle[...] + other[...], centre(bg[...]))
     store_spectrum(held, 0, to_complex(right_product(rows_forward(row_e, row_o, ratio[...]), col_w)))
 
-    for k in range(0, weights.shape[0], 2):
+    def filtered(k):
         planes = []
         a, b, c, d = load_spectrum(held, 0)
         for i in range(2):
@@ -297,7 +301,15 @@
             high, low = split(plane)
             both = dot(high, col_i[...])
             planes.append(both[:, :LANES] + (both[:, LANES:] + dot(low, col_i[:, :LANES])))
-        pair = rows_inverse(inv_e, inv_o, jnp.concatenate(planes, axis=1), total.shape[0])
+        return jnp.concatenate(planes, axis=1)
+
+    components = weights.shape[0]
+    ahead = filtered(0)
+    for k in range(0, components, 2):
+        planes = ahead
+        if k + 2 < components:
+            ahead = filtered(k + 2)
+        pair = rows_inverse(inv_e, inv_o, planes, total.shape[0])
         sums = (
             side_columns(weights.at[k], side) * pair[:, :LANES]
             + side_columns(weights.at[k + 1], side) * pair[:, LANES:]

time: 20.7 us -> 19.4 us (0.937)
  Pallas kernels: 14.1 us -> 12.8 us
    pallas_call x4, Pallas kernels: 14.1 us -> 12.8 us  [call(): pl.pallas_call(kernel, in_specs=[pl.BlockSpec(memory_space=space)] * len(...]
  transfers between devices with their start and end apart: 3 -> 3, of which waited for: 2 -> 2; matrix products, arithmetic and copies ran while one was open for 0% -> 0% of each run, Pallas kernels for 26% -> 24%
where the time goes in v2:
time: 19.4 us; the launch traced here: 19.2 us
  Pallas kernels  12.8 us (66%)
  starting transfers between devices  5.09 us (26%)
  waiting for transfers between devices  1.27 us (7%)
    pallas_call x4, Pallas kernels, call(): pl.pallas_call(kernel, in_specs=[pl.BlockSpec(memory_space=space)] * len(...  12.8 us
    ppermute x1, starting transfers between devices, local(): lax.ppermute(packed_i, 'col', within)  4.33 us
    ppermute x1, waiting for transfers between devices, local(): lax.ppermute(packed_i, 'col', within)  0.91 us
    ppermute x1, starting transfers between devices, local(): received_o = lax.ppermute(edge_o, 'col', between)  0.68 us
  transfers between devices with their start and end apart: 3, of which 2 were waited for; matrix products, arithmetic and copies ran while one was open for 0% of the time, Pallas kernels for 24%

profile of v2, /device:TPU:0, one launch (start us, length us, event | category | flops | bytes accessed | tf_op | source)
XLA Modules:
  0.0 19.2 jit_solution(11335874762986878347)
XLA Ops:
  0.0 5.1 %outer_blur.1 = (f32[8,320,256]{2,1,0:T(8,128)S(1)}, f32[256,256]{1,0:T(8,128)S(1)}, f32[256,128]{1,0:T(8,128)S(1)}, bf16[160,480]{1,0:T(8,128)(2,1)S(1)}, bf16[...) custom-call(f32[129,8,129]{2,1,0:T(8,128)} %bitcast.1, ...), custom_call_target="tpu_custom_call" | custom-call | flops 30198988 | bytes 54886 | tf_op jit(solution)/shard_map/outer_blur/pallas_call | solution.py:343
  5.1 0.7 %collective-permute-start = (f32[256,256]{1,0:T(8,128)S(1)}, f32[256,256]{1,0:T(8,128)S(1)}, u32[]{:S(2)}, u32[]{:S(2)}) collective-permute-start(f32[256,256]{1,0:T(8,128)S(1)} %get-tuple-element.30.refs_8_), channel_id=1, source_target_pairs={{1,2},{3,4},{5,6},{7,8},{9,10},{11,12},{13,14},{2,1},{4,3},{6,5},{... | collective-permute-start | bytes 786440 | tf_op jit(solution)/shard_map/ppermute | solution.py:409
  5.8 0.0 copy-start
  5.8 0.0 copy-start.1
  5.8 0.0 copy-start.2
  5.8 2.1 %inner_blur.1 = (f32[256,128]{1,0:T(8,128)S(1)}, f32[256,128]{1,0:T(8,128)S(1)}, f32[256,128]{1,0:T(8,128)S(1)}) custom-call(f32[256,256]{1,0:T(8,128)S(1)} %get-tuple-element.23.est.refs_0_, f32[256,256]{1,0:T(8,128)S(1)} %get-tuple-element.24.obs.refs_1_, f32[256,256]{1,0:T(8,128)S(1)} %get-tuple-element.25.bg.refs_2_, ...), custom_call_target="tpu_custom_call" | custom-call | flops 15099494 | bytes 72335 | tf_op jit(solution)/shard_map/inner_blur/pallas_call | solution.py:343
  7.9 4.3 %collective-permute-start.2 = (f32[256,128]{1,0:T(8,128)S(1)}, f32[256,128]{1,0:T(8,128)S(1)}, u32[]{:S(2)}, u32[]{:S(2)}) collective-permute-start(f32[256,128]{1,0:T(8,128)S(1)} %get-tuple-element.40), channel_id=1, source_target_pairs={{0,1},{1,0},{2,3},{3,2},{4,5},{5,4},{6,7},{7,6},{8,9},{9,8},{10,11... | collective-permute-start | bytes 393224 | tf_op jit(solution)/shard_map/ppermute | solution.py:415
  12.3 0.1 collective-permute-start.1
  12.3 0.9 %collective-permute-done.2.refs_10_ = f32[256,128]{1,0:T(8,128)S(1)} collective-permute-done((f32[256,128]{1,0:T(8,128)S(1)}, f32[256,128]{1,0:T(8,128)S(1)}, u32[]{:S(2)}, u32[]{:S(2)}) %collective-permute-start.2) | collective-permute-done | bytes 131104 | tf_op jit(solution)/shard_map/ppermute | solution.py:415
  13.2 0.4 %collective-permute-done.1.refs_9_ = f32[256,128]{1,0:T(8,128)S(1)} collective-permute-done((f32[256,128]{1,0:T(8,128)S(1)}, f32[256,128]{1,0:T(8,128)S(1)}, u32[]{:S(2)}, u32[]{:S(2)}) %collective-permute-start.1) | collective-permute-done | bytes 131104 | tf_op jit(solution)/shard_map/ppermute | solution.py:415
  13.6 0.0 copy-done
  13.6 0.0 copy-done.1
  13.6 0.0 copy-done.2
  13.6 2.5 %inner_correct.1.refs_12_ = f32[256,128]{1,0:T(8,128)S(1)} custom-call(f32[256,256]{1,0:T(8,128)S(1)} %get-tuple-element.23.est.refs_0_, f32[256,256]{1,0:T(8,128)S(1)} %get-tuple-element.24.obs.refs_1_, f32[256,256]{1,0:T(8,128)S(1)} %get-tuple-element.25.bg.refs_2_, f32[256,256]{1,0:T(8,128)S(1)} %copy-done.1, ...), custom_call_target="tpu_custom_call" | custom-call | flops 15099494 | bytes 80855 | tf_op jit(solution)/shard_map/inner_correct/pallas_call | solution.py:343
  16.1 0.0 collective-permute-done.refs_9_
  16.1 3.1 %outer_correct.1 = f32[256,256]{1,0:T(8,128)} custom-call(f32[256,256]{1,0:T(8,128)S(1)} %get-tuple-element.23.est.refs_0_, f32[256,256]{1,0:T(8,128)S(1)} %get-tuple-element.24.obs.refs_1_, f32[256,256]{1,0:T(8,128)S(1)} %get-tuple-element.25.bg.refs_2_, f32[256,256]{1,0:T(8,128)S(1)} %copy-done.1, s32[256,256]{1,0:T(8,128)S(1)} %get-tuple-element.26.valid.refs_4_, ...), custom_call_target="tpu_custom_call" | custom-call | flops 15099494 | bytes 83476 | tf_op jit(solution)/shard_map/outer_correct/pallas_call | solution.py:343
Async XLA Ops:
  5.1 11.0 %collective-permute-start = (f32[256,256]{1,0:T(8,128)S(1)}, f32[256,256]{1,0:T(8,128)S(1)}, u32[]{:S(2)}, u32[]{:S(2)}) collective-permute-start(f32[256,256]{1,0:T(8,128)S(1)} %get-tuple-element.30.refs_8_), channel_id=1, source_target_pairs={{1,2},{3,4},{5,6},{7,8},{9,10},{11,12},{13,14},{2,1},{4,3},{6,5},{... | collective-permute-start | bytes 786440 | tf_op jit(solution)/shard_map/ppermute | solution.py:409
  5.8 7.8 %copy-start = (bf16[768,256]{1,0:T(8,128)(2,1)S(1)}, bf16[768,256]{1,0:T(8,128)(2,1)}, u32[]{:S(2)}) copy-start(bf16[768,256]{1,0:T(8,128)(2,1)} %constant.30.clone.refs_15_) | copy-start | bytes 1179652
  5.8 7.8 %copy-start.1 = (f32[256,256]{1,0:T(8,128)S(1)}, f32[256,256]{1,0:T(8,128)}, u32[]{:S(2)}) copy-start(f32[256,256]{1,0:T(8,128)} %refs_3_.4) | copy-start | bytes 786436
  5.8 7.8 %copy-start.2 = (bf16[256,256]{1,0:T(8,128)(2,1)S(1)}, bf16[256,256]{1,0:T(8,128)(2,1)}, u32[]{:S(2)}) copy-start(bf16[256,256]{1,0:T(8,128)(2,1)} %constant.32.clone.refs_18_) | copy-start | bytes 393220
  7.9 5.3 %collective-permute-start.2 = (f32[256,128]{1,0:T(8,128)S(1)}, f32[256,128]{1,0:T(8,128)S(1)}, u32[]{:S(2)}, u32[]{:S(2)}) collective-permute-start(f32[256,128]{1,0:T(8,128)S(1)} %get-tuple-element.40), channel_id=1, source_target_pairs={{0,1},{1,0},{2,3},{3,2},{4,5},{5,4},{6,7},{7,6},{8,9},{9,8},{10,11... | collective-permute-start | bytes 393224 | tf_op jit(solution)/shard_map/ppermute | solution.py:415
  12.3 1.3 %collective-permute-start.1 = (f32[256,128]{1,0:T(8,128)S(1)}, f32[256,128]{1,0:T(8,128)S(1)}, u32[]{:S(2)}, u32[]{:S(2)}) collective-permute-start(f32[256,128]{1,0:T(8,128)S(1)} %get-tuple-element.39.refs_8_), channel_id=1, source_target_pairs={{0,1},{1,0},{2,3},{3,2},{4,5},{5,4},{6,7},{7,6},{8,9},{9,8},{10,11... | collective-permute-start | bytes 393224 | tf_op jit(solution)/shard_map/ppermute | solution.py:415

commit v3 on v2

--- a/solution.py
+++ b/solution.py
@@ -11,6 +11,7 @@
 COVER = 8
 LANES = 128
 VMEM_MIB = 32
+CHUNKS = 2
 BF16 = jnp.bfloat16
 F32 = jnp.float32
 
@@ -174,8 +175,8 @@
 
 
 def blur_end(side, obs, bg, valid, counts, inv_e, inv_o, col_i, total, edge, packed, middle, window):
-    plane = right_product(from_complex(*load_spectrum(total, 0)), col_i)
-    window[...] = rows_inverse(inv_e, inv_o, plane, window.shape[0])
+    plane = rows_inverse(inv_e, inv_o, from_complex(*load_spectrum(total, 0)), window.shape[0])
+    window[...] = right_product(plane, col_i)
     edge[...] = side_columns(window, side)
     middle[...] = side_columns(window, 1 - side)
     num = numerator(obs, valid, counts)
@@ -270,27 +271,34 @@
     side = side_of(outer)
     lane = lax.broadcasted_iota(jnp.int32, (1, LANES), 1)
     left = lane < LANES // 2
-    num = numerator(obs[...], valid[...], counts[...])
-
-    def centre(own):
-        return jnp.where(left, swap(own[:, :LANES]), swap(own[:, LANES:]))
-
-    def at_edge(own):
-        return swap(jnp.where(side == 0, own[:, :LANES], own[:, LANES:]))
+    from_other = (lane >= LANES // 2) == (side == 1)
 
     def divided(num, blurred, back):
         return jnp.where(num > 0.0, num / (blurred + back), 0.0)
 
-    packed = packed[...]
-    turned = swap(packed)
-    from_other = (lane >= LANES // 2) == (side == 1)
-    edge_num = jnp.where(from_other, jnp.where(side == 0, packed, turned), at_edge(num))
-    edge_back = jnp.where(from_other, jnp.where(side == 0, turned, packed), at_edge(bg[...]))
     first = pl.ds(pl.multiple_of(side * LANES, LANES), LANES)
     second = pl.ds(pl.multiple_of((1 - side) * LANES, LANES), LANES)
-    ratio[:, first] = divided(edge_num, edge[...] + received[...], edge_back)
-    ratio[:, second] = divided(centre(num), middle[...] + other[...], centre(bg[...]))
-    store_spectrum(held, 0, to_complex(right_product(rows_forward(row_e, row_o, ratio[...]), col_w)))
+    count = obs.shape[0] // CHUNKS
+    pieces = []
+    for start in range(0, obs.shape[0], count):
+        some = slice(start, start + count)
+        num, back = numerator(obs[some], valid[some], counts[some]), bg[some]
+
+        def centre(own):
+            return jnp.where(left, swap(own[:, :LANES]), swap(own[:, LANES:]))
+
+        def at_edge(own):
+            return swap(jnp.where(side == 0, own[:, :LANES], own[:, LANES:]))
+
+        straight = packed[some]
+        turned = swap(straight)
+        edge_num = jnp.where(from_other, jnp.where(side == 0, straight, turned), at_edge(num))
+        edge_back = jnp.where(from_other, jnp.where(side == 0, turned, straight), at_edge(back))
+        ratio[some, first] = divided(edge_num, edge[some] + received[some], edge_back)
+        ratio[some, second] = divided(centre(num), middle[some] + other[some], centre(back))
+        pieces.append(right_product(ratio[some], col_w))
+    turned_ratio = jnp.concatenate(pieces, axis=0)
+    store_spectrum(held, 0, to_complex(rows_forward(row_e, row_o, turned_ratio)))
 
     def filtered(k):
         planes = []

time: 19.4 us -> 18.8 us (0.969)
  Pallas kernels: 12.8 us -> 12.2 us
    pallas_call x4, Pallas kernels: 12.8 us -> 12.2 us  [call(): pl.pallas_call(kernel, in_specs=[pl.BlockSpec(memory_space=space)] * len(...]
  transfers between devices with their start and end apart: 3 -> 3, of which waited for: 2 -> 2; matrix products, arithmetic and copies ran while one was open for 0% -> 0% of each run, Pallas kernels for 24% -> 23%
where the time goes in v3:
time: 18.8 us; the launch traced here: 18.6 us
  Pallas kernels  12.2 us (65%)
  starting transfers between devices  5.08 us (27%)
  waiting for transfers between devices  1.27 us (7%)
    pallas_call x4, Pallas kernels, call(): pl.pallas_call(kernel, in_specs=[pl.BlockSpec(memory_space=space)] * len(...  12.2 us
    ppermute x1, starting transfers between devices, local(): lax.ppermute(packed_i, 'col', within)  4.32 us
    ppermute x1, waiting for transfers between devices, local(): lax.ppermute(packed_i, 'col', within)  0.91 us
    ppermute x1, starting transfers between devices, local(): received_o = lax.ppermute(edge_o, 'col', between)  0.68 us
  transfers between devices with their start and end apart: 3, of which 2 were waited for; matrix products, arithmetic and copies ran while one was open for 0% of the time, Pallas kernels for 23%

profile of v3, /device:TPU:0, one launch (start us, length us, event | category | flops | bytes accessed | tf_op | source)
XLA Modules:
  0.0 18.6 jit_solution(8695273535078294239)
XLA Ops:
  0.0 5.0 %outer_blur.1 = (f32[8,320,256]{2,1,0:T(8,128)S(1)}, f32[256,256]{1,0:T(8,128)S(1)}, f32[256,128]{1,0:T(8,128)S(1)}, bf16[160,480]{1,0:T(8,128)(2,1)S(1)}, bf16[...) custom-call(f32[129,8,129]{2,1,0:T(8,128)} %bitcast.1, ...), custom_call_target="tpu_custom_call" | custom-call | flops 30198988 | bytes 54886 | tf_op jit(solution)/shard_map/outer_blur/pallas_call | solution.py:351
  5.0 0.7 %collective-permute-start = (f32[256,256]{1,0:T(8,128)S(1)}, f32[256,256]{1,0:T(8,128)S(1)}, u32[]{:S(2)}, u32[]{:S(2)}) collective-permute-start(f32[256,256]{1,0:T(8,128)S(1)} %get-tuple-element.30.refs_8_), channel_id=1, source_target_pairs={{1,2},{3,4},{5,6},{7,8},{9,10},{11,12},{13,14},{2,1},{4,3},{6,5},{... | collective-permute-start | bytes 786440 | tf_op jit(solution)/shard_map/ppermute | solution.py:417
  5.7 0.0 copy-start
  5.7 0.0 copy-start.1
  5.7 0.0 copy-start.2
  5.7 2.1 %inner_blur.1 = (f32[256,128]{1,0:T(8,128)S(1)}, f32[256,128]{1,0:T(8,128)S(1)}, f32[256,128]{1,0:T(8,128)S(1)}) custom-call(f32[256,256]{1,0:T(8,128)S(1)} %get-tuple-element.23.est.refs_0_, f32[256,256]{1,0:T(8,128)S(1)} %get-tuple-element.24.obs.refs_1_, f32[256,256]{1,0:T(8,128)S(1)} %get-tuple-element.25.bg.refs_2_, ...), custom_call_target="tpu_custom_call" | custom-call | flops 15099494 | bytes 72335 | tf_op jit(solution)/shard_map/inner_blur/pallas_call | solution.py:351
  7.9 4.3 %collective-permute-start.2 = (f32[256,128]{1,0:T(8,128)S(1)}, f32[256,128]{1,0:T(8,128)S(1)}, u32[]{:S(2)}, u32[]{:S(2)}) collective-permute-start(f32[256,128]{1,0:T(8,128)S(1)} %get-tuple-element.40), channel_id=1, source_target_pairs={{0,1},{1,0},{2,3},{3,2},{4,5},{5,4},{6,7},{7,6},{8,9},{9,8},{10,11... | collective-permute-start | bytes 393224 | tf_op jit(solution)/shard_map/ppermute | solution.py:423
  12.2 0.1 collective-permute-start.1
  12.3 0.9 %collective-permute-done.2.refs_10_ = f32[256,128]{1,0:T(8,128)S(1)} collective-permute-done((f32[256,128]{1,0:T(8,128)S(1)}, f32[256,128]{1,0:T(8,128)S(1)}, u32[]{:S(2)}, u32[]{:S(2)}) %collective-permute-start.2) | collective-permute-done | bytes 131104 | tf_op jit(solution)/shard_map/ppermute | solution.py:423
  13.2 0.4 %collective-permute-done.1.refs_9_ = f32[256,128]{1,0:T(8,128)S(1)} collective-permute-done((f32[256,128]{1,0:T(8,128)S(1)}, f32[256,128]{1,0:T(8,128)S(1)}, u32[]{:S(2)}, u32[]{:S(2)}) %collective-permute-start.1) | collective-permute-done | bytes 131104 | tf_op jit(solution)/shard_map/ppermute | solution.py:423
  13.5 0.0 copy-done
  13.5 0.0 copy-done.1
  13.5 0.0 copy-done.2
  13.5 2.2 %inner_correct.1.refs_12_ = f32[256,128]{1,0:T(8,128)S(1)} custom-call(f32[256,256]{1,0:T(8,128)S(1)} %get-tuple-element.23.est.refs_0_, f32[256,256]{1,0:T(8,128)S(1)} %get-tuple-element.24.obs.refs_1_, f32[256,256]{1,0:T(8,128)S(1)} %get-tuple-element.25.bg.refs_2_, f32[256,256]{1,0:T(8,128)S(1)} %copy-done.1, ...), custom_call_target="tpu_custom_call" | custom-call | flops 15099494 | bytes 80855 | tf_op jit(solution)/shard_map/inner_correct/pallas_call | solution.py:351
  15.7 0.0 collective-permute-done.refs_9_
  15.7 2.9 %outer_correct.1 = f32[256,256]{1,0:T(8,128)} custom-call(f32[256,256]{1,0:T(8,128)S(1)} %get-tuple-element.23.est.refs_0_, f32[256,256]{1,0:T(8,128)S(1)} %get-tuple-element.24.obs.refs_1_, f32[256,256]{1,0:T(8,128)S(1)} %get-tuple-element.25.bg.refs_2_, f32[256,256]{1,0:T(8,128)S(1)} %copy-done.1, s32[256,256]{1,0:T(8,128)S(1)} %get-tuple-element.26.valid.refs_4_, ...), custom_call_target="tpu_custom_call" | custom-call | flops 15099494 | bytes 83476 | tf_op jit(solution)/shard_map/outer_correct/pallas_call | solution.py:351
Async XLA Ops:
  5.0 10.7 %collective-permute-start = (f32[256,256]{1,0:T(8,128)S(1)}, f32[256,256]{1,0:T(8,128)S(1)}, u32[]{:S(2)}, u32[]{:S(2)}) collective-permute-start(f32[256,256]{1,0:T(8,128)S(1)} %get-tuple-element.30.refs_8_), channel_id=1, source_target_pairs={{1,2},{3,4},{5,6},{7,8},{9,10},{11,12},{13,14},{2,1},{4,3},{6,5},{... | collective-permute-start | bytes 786440 | tf_op jit(solution)/shard_map/ppermute | solution.py:417
  5.7 7.8 %copy-start = (bf16[768,256]{1,0:T(8,128)(2,1)S(1)}, bf16[768,256]{1,0:T(8,128)(2,1)}, u32[]{:S(2)}) copy-start(bf16[768,256]{1,0:T(8,128)(2,1)} %constant.30.clone.refs_15_) | copy-start | bytes 1179652
  5.7 7.8 %copy-start.1 = (f32[256,256]{1,0:T(8,128)S(1)}, f32[256,256]{1,0:T(8,128)}, u32[]{:S(2)}) copy-start(f32[256,256]{1,0:T(8,128)} %refs_3_.4) | copy-start | bytes 786436
  5.7 7.8 %copy-start.2 = (bf16[256,256]{1,0:T(8,128)(2,1)S(1)}, bf16[256,256]{1,0:T(8,128)(2,1)}, u32[]{:S(2)}) copy-start(bf16[256,256]{1,0:T(8,128)(2,1)} %constant.32.clone.refs_18_) | copy-start | bytes 393220
  7.9 5.3 %collective-permute-start.2 = (f32[256,128]{1,0:T(8,128)S(1)}, f32[256,128]{1,0:T(8,128)S(1)}, u32[]{:S(2)}, u32[]{:S(2)}) collective-permute-start(f32[256,128]{1,0:T(8,128)S(1)} %get-tuple-element.40), channel_id=1, source_target_pairs={{0,1},{1,0},{2,3},{3,2},{4,5},{5,4},{6,7},{7,6},{8,9},{9,8},{10,11... | collective-permute-start | bytes 393224 | tf_op jit(solution)/shard_map/ppermute | solution.py:423
  12.2 1.3 %collective-permute-start.1 = (f32[256,128]{1,0:T(8,128)S(1)}, f32[256,128]{1,0:T(8,128)S(1)}, u32[]{:S(2)}, u32[]{:S(2)}) collective-permute-start(f32[256,128]{1,0:T(8,128)S(1)} %get-tuple-element.39.refs_8_), channel_id=1, source_target_pairs={{0,1},{1,0},{2,3},{3,2},{4,5},{5,4},{6,7},{7,6},{8,9},{9,8},{10,11... | collective-permute-start | bytes 393224 | tf_op jit(solution)/shard_map/ppermute | solution.py:423

commit v4 on v3

--- a/solution.py
+++ b/solution.py
@@ -151,8 +151,8 @@
 def blur_pairs(est_half, weight_of, spectrum_of, components, row_e, row_o, col_f, total):
     def ahead(k):
         pair = jnp.concatenate([weight_of(k + i) * est_half for i in range(2)], axis=1)
-        rows = rows_forward(row_e, row_o, pair)
-        return rows, [spectrum_of(k + i) for i in range(2)]
+        spectra = [spectrum_of(k + i) for i in range(2)]
+        return rows_forward(row_e, row_o, pair), spectra
 
     coming = ahead(0)
     for k in range(0, components, 2):
@@ -215,12 +215,17 @@
     copies[1].wait()
     above, below = kernels[centre + 1:], [kernels[i:i + 1] for i in range(centre - 1, -1, -1)]
     below = jnp.concatenate(below, axis=0)
-    folded = jnp.concatenate([above - below, kernels[centre:centre + 1], above + below], axis=0)
-    plane = right_product(folded.reshape(size * components, size), col_h)
+    turned = (above - below, jnp.concatenate([kernels[centre:centre + 1], above + below], axis=0))
+    start = 0
+    for folded in turned:
+        flat = folded.reshape(-1, size)
+        plane = right_product(flat, col_h)
+        for part, ref in enumerate(columns):
+            ref[start:start + len(flat)] = plane[:, part * LANES:(part + 1) * LANES]
+        start += len(flat)
     empty = (odds + evens - size) * components
-    for part, ref in enumerate(columns):
-        ref[:size * components] = plane[:, part * LANES:(part + 1) * LANES]
-        ref[size * components:] = jnp.zeros((empty, LANES), F32)
+    for ref in columns:
+        ref[start:] = jnp.zeros((empty, LANES), F32)
     for copy in copies[2:9]:
         copy.wait()
     for copy in copies[9:]:

time: 18.8 us -> 18.4 us (0.979)
  Pallas kernels: 12.2 us -> 11.8 us
    pallas_call x4, Pallas kernels: 12.2 us -> 11.8 us  [call(): pl.pallas_call(kernel, in_specs=[pl.BlockSpec(memory_space=space)] * len(...]
  transfers between devices with their start and end apart: 3 -> 3, of which waited for: 2 -> 2; matrix products, arithmetic and copies ran while one was open for 0% -> 0% of each run, Pallas kernels for 23% -> 24%
where the time goes in v4:
time: 18.4 us; the launch traced here: 18.2 us
  Pallas kernels  11.8 us (64%)
  starting transfers between devices  5.09 us (28%)
  waiting for transfers between devices  1.27 us (7%)
    pallas_call x4, Pallas kernels, call(): pl.pallas_call(kernel, in_specs=[pl.BlockSpec(memory_space=space)] * len(...  11.8 us
    ppermute x1, starting transfers between devices, local(): lax.ppermute(packed_i, 'col', within)  4.34 us
    ppermute x1, waiting for transfers between devices, local(): lax.ppermute(packed_i, 'col', within)  0.91 us
    ppermute x1, starting transfers between devices, local(): received_o = lax.ppermute(edge_o, 'col', between)  0.68 us
  transfers between devices with their start and end apart: 3, of which 2 were waited for; matrix products, arithmetic and copies ran while one was open for 0% of the time, Pallas kernels for 24%

profile of v4, /device:TPU:0, one launch (start us, length us, event | category | flops | bytes accessed | tf_op | source)
XLA Modules:
  0.0 18.2 jit_solution(10583921890943926625)
XLA Ops:
  0.0 4.6 %outer_blur.1 = (f32[8,320,256]{2,1,0:T(8,128)S(1)}, f32[256,256]{1,0:T(8,128)S(1)}, f32[256,128]{1,0:T(8,128)S(1)}, bf16[160,480]{1,0:T(8,128)(2,1)S(1)}, bf16[...) custom-call(f32[129,8,129]{2,1,0:T(8,128)} %bitcast.1, ...), custom_call_target="tpu_custom_call" | custom-call | flops 30198988 | bytes 54886 | tf_op jit(solution)/shard_map/outer_blur/pallas_call | solution.py:356
  4.6 0.7 %collective-permute-start = (f32[256,256]{1,0:T(8,128)S(1)}, f32[256,256]{1,0:T(8,128)S(1)}, u32[]{:S(2)}, u32[]{:S(2)}) collective-permute-start(f32[256,256]{1,0:T(8,128)S(1)} %get-tuple-element.30.refs_8_), channel_id=1, source_target_pairs={{1,2},{3,4},{5,6},{7,8},{9,10},{11,12},{13,14},{2,1},{4,3},{6,5},{... | collective-permute-start | bytes 786440 | tf_op jit(solution)/shard_map/ppermute | solution.py:422
  5.3 0.0 copy-start
  5.3 0.0 copy-start.1
  5.3 0.0 copy-start.2
  5.4 2.1 %inner_blur.1 = (f32[256,128]{1,0:T(8,128)S(1)}, f32[256,128]{1,0:T(8,128)S(1)}, f32[256,128]{1,0:T(8,128)S(1)}) custom-call(f32[256,256]{1,0:T(8,128)S(1)} %get-tuple-element.23.est.refs_0_, f32[256,256]{1,0:T(8,128)S(1)} %get-tuple-element.24.obs.refs_1_, f32[256,256]{1,0:T(8,128)S(1)} %get-tuple-element.25.bg.refs_2_, ...), custom_call_target="tpu_custom_call" | custom-call | flops 15099494 | bytes 72335 | tf_op jit(solution)/shard_map/inner_blur/pallas_call | solution.py:356
  7.5 4.3 %collective-permute-start.2 = (f32[256,128]{1,0:T(8,128)S(1)}, f32[256,128]{1,0:T(8,128)S(1)}, u32[]{:S(2)}, u32[]{:S(2)}) collective-permute-start(f32[256,128]{1,0:T(8,128)S(1)} %get-tuple-element.40), channel_id=1, source_target_pairs={{0,1},{1,0},{2,3},{3,2},{4,5},{5,4},{6,7},{7,6},{8,9},{9,8},{10,11... | collective-permute-start | bytes 393224 | tf_op jit(solution)/shard_map/ppermute | solution.py:428
  11.8 0.1 collective-permute-start.1
  11.9 0.9 %collective-permute-done.2.refs_10_ = f32[256,128]{1,0:T(8,128)S(1)} collective-permute-done((f32[256,128]{1,0:T(8,128)S(1)}, f32[256,128]{1,0:T(8,128)S(1)}, u32[]{:S(2)}, u32[]{:S(2)}) %collective-permute-start.2) | collective-permute-done | bytes 131104 | tf_op jit(solution)/shard_map/ppermute | solution.py:428
  12.8 0.4 %collective-permute-done.1.refs_9_ = f32[256,128]{1,0:T(8,128)S(1)} collective-permute-done((f32[256,128]{1,0:T(8,128)S(1)}, f32[256,128]{1,0:T(8,128)S(1)}, u32[]{:S(2)}, u32[]{:S(2)}) %collective-permute-start.1) | collective-permute-done | bytes 131104 | tf_op jit(solution)/shard_map/ppermute | solution.py:428
  13.2 0.0 copy-done
  13.2 0.0 copy-done.1
  13.2 0.0 copy-done.2
  13.2 2.2 %inner_correct.1.refs_12_ = f32[256,128]{1,0:T(8,128)S(1)} custom-call(f32[256,256]{1,0:T(8,128)S(1)} %get-tuple-element.23.est.refs_0_, f32[256,256]{1,0:T(8,128)S(1)} %get-tuple-element.24.obs.refs_1_, f32[256,256]{1,0:T(8,128)S(1)} %get-tuple-element.25.bg.refs_2_, f32[256,256]{1,0:T(8,128)S(1)} %copy-done.1, ...), custom_call_target="tpu_custom_call" | custom-call | flops 15099494 | bytes 80855 | tf_op jit(solution)/shard_map/inner_correct/pallas_call | solution.py:356
  15.4 0.0 collective-permute-done.refs_9_
  15.4 2.9 %outer_correct.1 = f32[256,256]{1,0:T(8,128)} custom-call(f32[256,256]{1,0:T(8,128)S(1)} %get-tuple-element.23.est.refs_0_, f32[256,256]{1,0:T(8,128)S(1)} %get-tuple-element.24.obs.refs_1_, f32[256,256]{1,0:T(8,128)S(1)} %get-tuple-element.25.bg.refs_2_, f32[256,256]{1,0:T(8,128)S(1)} %copy-done.1, s32[256,256]{1,0:T(8,128)S(1)} %get-tuple-element.26.valid.refs_4_, ...), custom_call_target="tpu_custom_call" | custom-call | flops 15099494 | bytes 83476 | tf_op jit(solution)/shard_map/outer_correct/pallas_call | solution.py:356
Async XLA Ops:
  4.6 10.7 %collective-permute-start = (f32[256,256]{1,0:T(8,128)S(1)}, f32[256,256]{1,0:T(8,128)S(1)}, u32[]{:S(2)}, u32[]{:S(2)}) collective-permute-start(f32[256,256]{1,0:T(8,128)S(1)} %get-tuple-element.30.refs_8_), channel_id=1, source_target_pairs={{1,2},{3,4},{5,6},{7,8},{9,10},{11,12},{13,14},{2,1},{4,3},{6,5},{... | collective-permute-start | bytes 786440 | tf_op jit(solution)/shard_map/ppermute | solution.py:422
  5.3 7.8 %copy-start = (bf16[768,256]{1,0:T(8,128)(2,1)S(1)}, bf16[768,256]{1,0:T(8,128)(2,1)}, u32[]{:S(2)}) copy-start(bf16[768,256]{1,0:T(8,128)(2,1)} %constant.30.clone.refs_15_) | copy-start | bytes 1179652
  5.3 7.8 %copy-start.1 = (f32[256,256]{1,0:T(8,128)S(1)}, f32[256,256]{1,0:T(8,128)}, u32[]{:S(2)}) copy-start(f32[256,256]{1,0:T(8,128)} %refs_3_.4) | copy-start | bytes 786436
  5.3 7.8 %copy-start.2 = (bf16[256,256]{1,0:T(8,128)(2,1)S(1)}, bf16[256,256]{1,0:T(8,128)(2,1)}, u32[]{:S(2)}) copy-start(bf16[256,256]{1,0:T(8,128)(2,1)} %constant.32.clone.refs_18_) | copy-start | bytes 393220
  7.5 5.3 %collective-permute-start.2 = (f32[256,128]{1,0:T(8,128)S(1)}, f32[256,128]{1,0:T(8,128)S(1)}, u32[]{:S(2)}, u32[]{:S(2)}) collective-permute-start(f32[256,128]{1,0:T(8,128)S(1)} %get-tuple-element.40), channel_id=1, source_target_pairs={{0,1},{1,0},{2,3},{3,2},{4,5},{5,4},{6,7},{7,6},{8,9},{9,8},{10,11... | collective-permute-start | bytes 393224 | tf_op jit(solution)/shard_map/ppermute | solution.py:428
  11.8 1.3 %collective-permute-start.1 = (f32[256,128]{1,0:T(8,128)S(1)}, f32[256,128]{1,0:T(8,128)S(1)}, u32[]{:S(2)}, u32[]{:S(2)}) collective-permute-start(f32[256,128]{1,0:T(8,128)S(1)} %get-tuple-element.39.refs_8_), channel_id=1, source_target_pairs={{0,1},{1,0},{2,3},{3,2},{4,5},{5,4},{6,7},{7,6},{8,9},{9,8},{10,11... | collective-permute-start | bytes 393224 | tf_op jit(solution)/shard_map/ppermute | solution.py:428

commit v5 on v4

--- a/solution.py
+++ b/solution.py
@@ -101,10 +101,12 @@
     return jnp.concatenate([jnp.where(row == 0, first, values[:8]), values[8:]], axis=0)
 
 
-def to_complex(plane):
+def to_complex(plane, with_first=True):
     half = plane.shape[0] // 2
     cc, cs = plane[:half, :LANES], plane[:half, LANES:]
     sc, ss = plane[half:, :LANES], plane[half:, LANES:]
+    if not with_first:
+        return cc - ss, cs + sc, cc + ss, cs - sc
     return (
         fix_first(cc[:8], cc - ss), fix_first(cs[:8], cs + sc),
         fix_first(sc[:8], cc + ss), fix_first(ss[:8], cs - sc),
@@ -159,13 +161,24 @@
         rows, spectra = coming
         if k + 2 < components:
             coming = ahead(k + 2)
-        sums = None
-        for i in range(2):
-            fa, fb, fc, fd = to_complex(right_product(rows[:, i * LANES:(i + 1) * LANES], col_f))
-            ha, hb, hc, hd = spectra[i]
-            terms = (fa * ha - fb * hb, fa * hb + fb * ha, fc * hc - fd * hd, fc * hd + fd * hc)
-            sums = terms if sums is None else tuple(s + t for s, t in zip(sums, terms))
-        accumulate(total, k == 0, sums)
+        half = rows.shape[0] // 2
+        step = half // 2
+        for start in (0, step):
+            sums = None
+            for i in range(2):
+                lanes = slice(i * LANES, (i + 1) * LANES)
+                part = jnp.concatenate(
+                    [rows[start:start + step, lanes], rows[half + start:half + start + step, lanes]], axis=0
+                )
+                fa, fb, fc, fd = to_complex(right_product(part, col_f), start == 0)
+                ha, hb, hc, hd = (h[start:start + step] for h in spectra[i])
+                terms = (fa * ha - fb * hb, fa * hb + fb * ha, fc * hc - fd * hd, fc * hd + fd * hc)
+                sums = terms if sums is None else tuple(s + t for s, t in zip(sums, terms))
+            upper, lower = slice(start, start + step), slice(half + start, half + start + step)
+            places = ((upper, 0), (upper, LANES), (lower, 0), (lower, LANES))
+            for (place, lane), value in zip(places, sums):
+                lanes = slice(lane, lane + LANES)
+                total[0, place, lanes] = value if k == 0 else total[0, place, lanes] + value
 
 
 def accumulate(ref, first, sums):

time: 18.4 us -> 18.2 us (0.989)
  Pallas kernels: 11.8 us -> 11.6 us
    pallas_call x4, Pallas kernels: 11.8 us -> 11.6 us  [call(): pl.pallas_call(kernel, in_specs=[pl.BlockSpec(memory_space=space)] * len(...]
  transfers between devices with their start and end apart: 3 -> 3, of which waited for: 2 -> 2; matrix products, arithmetic and copies ran while one was open for 0% -> 0% of each run, Pallas kernels for 24% -> 23%
where the time goes in v5:
time: 18.2 us; the launch traced here: 18 us
  Pallas kernels  11.6 us (64%)
  starting transfers between devices  5.08 us (28%)
  waiting for transfers between devices  1.27 us (7%)
    pallas_call x4, Pallas kernels, call(): pl.pallas_call(kernel, in_specs=[pl.BlockSpec(memory_space=space)] * len(...  11.6 us
    ppermute x1, starting transfers between devices, local(): lax.ppermute(packed_i, 'col', within)  4.32 us
    ppermute x1, waiting for transfers between devices, local(): lax.ppermute(packed_i, 'col', within)  0.91 us
    ppermute x1, starting transfers between devices, local(): received_o = lax.ppermute(edge_o, 'col', between)  0.68 us
  transfers between devices with their start and end apart: 3, of which 2 were waited for; matrix products, arithmetic and copies ran while one was open for 0% of the time, Pallas kernels for 23%

profile of v5, /device:TPU:0, one launch (start us, length us, event | category | flops | bytes accessed | tf_op | source)
XLA Modules:
  0.0 18.0 jit_solution(15116482887894001641)
XLA Ops:
  0.0 4.6 %outer_blur.1 = (f32[8,320,256]{2,1,0:T(8,128)S(1)}, f32[256,256]{1,0:T(8,128)S(1)}, f32[256,128]{1,0:T(8,128)S(1)}, bf16[160,480]{1,0:T(8,128)(2,1)S(1)}, bf16[...) custom-call(f32[129,8,129]{2,1,0:T(8,128)} %bitcast.1, ...), custom_call_target="tpu_custom_call" | custom-call | flops 30198988 | bytes 54886 | tf_op jit(solution)/shard_map/outer_blur/pallas_call | solution.py:369
  4.6 0.7 %collective-permute-start = (f32[256,256]{1,0:T(8,128)S(1)}, f32[256,256]{1,0:T(8,128)S(1)}, u32[]{:S(2)}, u32[]{:S(2)}) collective-permute-start(f32[256,256]{1,0:T(8,128)S(1)} %get-tuple-element.30.refs_8_), channel_id=1, source_target_pairs={{1,2},{3,4},{5,6},{7,8},{9,10},{11,12},{13,14},{2,1},{4,3},{6,5},{... | collective-permute-start | bytes 786440 | tf_op jit(solution)/shard_map/ppermute | solution.py:435
  5.3 0.0 copy-start
  5.3 0.0 copy-start.1
  5.3 0.0 copy-start.2
  5.3 1.9 %inner_blur.1 = (f32[256,128]{1,0:T(8,128)S(1)}, f32[256,128]{1,0:T(8,128)S(1)}, f32[256,128]{1,0:T(8,128)S(1)}) custom-call(f32[256,256]{1,0:T(8,128)S(1)} %get-tuple-element.23.est.refs_0_, f32[256,256]{1,0:T(8,128)S(1)} %get-tuple-element.24.obs.refs_1_, f32[256,256]{1,0:T(8,128)S(1)} %get-tuple-element.25.bg.refs_2_, ...), custom_call_target="tpu_custom_call" | custom-call | flops 15099494 | bytes 72335 | tf_op jit(solution)/shard_map/inner_blur/pallas_call | solution.py:369
  7.3 4.3 %collective-permute-start.2 = (f32[256,128]{1,0:T(8,128)S(1)}, f32[256,128]{1,0:T(8,128)S(1)}, u32[]{:S(2)}, u32[]{:S(2)}) collective-permute-start(f32[256,128]{1,0:T(8,128)S(1)} %get-tuple-element.40), channel_id=1, source_target_pairs={{0,1},{1,0},{2,3},{3,2},{4,5},{5,4},{6,7},{7,6},{8,9},{9,8},{10,11... | collective-permute-start | bytes 393224 | tf_op jit(solution)/shard_map/ppermute | solution.py:441
  11.6 0.1 collective-permute-start.1
  11.7 0.9 %collective-permute-done.2.refs_10_ = f32[256,128]{1,0:T(8,128)S(1)} collective-permute-done((f32[256,128]{1,0:T(8,128)S(1)}, f32[256,128]{1,0:T(8,128)S(1)}, u32[]{:S(2)}, u32[]{:S(2)}) %collective-permute-start.2) | collective-permute-done | bytes 131104 | tf_op jit(solution)/shard_map/ppermute | solution.py:441
  12.6 0.4 %collective-permute-done.1.refs_9_ = f32[256,128]{1,0:T(8,128)S(1)} collective-permute-done((f32[256,128]{1,0:T(8,128)S(1)}, f32[256,128]{1,0:T(8,128)S(1)}, u32[]{:S(2)}, u32[]{:S(2)}) %collective-permute-start.1) | collective-permute-done | bytes 131104 | tf_op jit(solution)/shard_map/ppermute | solution.py:441
  12.9 0.0 copy-done
  12.9 0.0 copy-done.1
  12.9 0.0 copy-done.2
  12.9 2.2 %inner_correct.1.refs_12_ = f32[256,128]{1,0:T(8,128)S(1)} custom-call(f32[256,256]{1,0:T(8,128)S(1)} %get-tuple-element.23.est.refs_0_, f32[256,256]{1,0:T(8,128)S(1)} %get-tuple-element.24.obs.refs_1_, f32[256,256]{1,0:T(8,128)S(1)} %get-tuple-element.25.bg.refs_2_, f32[256,256]{1,0:T(8,128)S(1)} %copy-done.1, ...), custom_call_target="tpu_custom_call" | custom-call | flops 15099494 | bytes 80855 | tf_op jit(solution)/shard_map/inner_correct/pallas_call | solution.py:369
  15.1 0.0 collective-permute-done.refs_9_
  15.1 2.9 %outer_correct.1 = f32[256,256]{1,0:T(8,128)} custom-call(f32[256,256]{1,0:T(8,128)S(1)} %get-tuple-element.23.est.refs_0_, f32[256,256]{1,0:T(8,128)S(1)} %get-tuple-element.24.obs.refs_1_, f32[256,256]{1,0:T(8,128)S(1)} %get-tuple-element.25.bg.refs_2_, f32[256,256]{1,0:T(8,128)S(1)} %copy-done.1, s32[256,256]{1,0:T(8,128)S(1)} %get-tuple-element.26.valid.refs_4_, ...), custom_call_target="tpu_custom_call" | custom-call | flops 15099494 | bytes 83476 | tf_op jit(solution)/shard_map/outer_correct/pallas_call | solution.py:369
Async XLA Ops:
  4.6 10.6 %collective-permute-start = (f32[256,256]{1,0:T(8,128)S(1)}, f32[256,256]{1,0:T(8,128)S(1)}, u32[]{:S(2)}, u32[]{:S(2)}) collective-permute-start(f32[256,256]{1,0:T(8,128)S(1)} %get-tuple-element.30.refs_8_), channel_id=1, source_target_pairs={{1,2},{3,4},{5,6},{7,8},{9,10},{11,12},{13,14},{2,1},{4,3},{6,5},{... | collective-permute-start | bytes 786440 | tf_op jit(solution)/shard_map/ppermute | solution.py:435
  5.3 7.7 %copy-start = (bf16[768,256]{1,0:T(8,128)(2,1)S(1)}, bf16[768,256]{1,0:T(8,128)(2,1)}, u32[]{:S(2)}) copy-start(bf16[768,256]{1,0:T(8,128)(2,1)} %constant.30.clone.refs_15_) | copy-start | bytes 1179652
  5.3 7.7 %copy-start.1 = (f32[256,256]{1,0:T(8,128)S(1)}, f32[256,256]{1,0:T(8,128)}, u32[]{:S(2)}) copy-start(f32[256,256]{1,0:T(8,128)} %refs_3_.4) | copy-start | bytes 786436
  5.3 7.6 %copy-start.2 = (bf16[256,256]{1,0:T(8,128)(2,1)S(1)}, bf16[256,256]{1,0:T(8,128)(2,1)}, u32[]{:S(2)}) copy-start(bf16[256,256]{1,0:T(8,128)(2,1)} %constant.32.clone.refs_18_) | copy-start | bytes 393220
  7.3 5.3 %collective-permute-start.2 = (f32[256,128]{1,0:T(8,128)S(1)}, f32[256,128]{1,0:T(8,128)S(1)}, u32[]{:S(2)}, u32[]{:S(2)}) collective-permute-start(f32[256,128]{1,0:T(8,128)S(1)} %get-tuple-element.40), channel_id=1, source_target_pairs={{0,1},{1,0},{2,3},{3,2},{4,5},{5,4},{6,7},{7,6},{8,9},{9,8},{10,11... | collective-permute-start | bytes 393224 | tf_op jit(solution)/shard_map/ppermute | solution.py:441
  11.6 1.3 %collective-permute-start.1 = (f32[256,128]{1,0:T(8,128)S(1)}, f32[256,128]{1,0:T(8,128)S(1)}, u32[]{:S(2)}, u32[]{:S(2)}) collective-permute-start(f32[256,128]{1,0:T(8,128)S(1)} %get-tuple-element.39.refs_8_), channel_id=1, source_target_pairs={{0,1},{1,0},{2,3},{3,2},{4,5},{5,4},{6,7},{7,6},{8,9},{9,8},{10,11... | collective-permute-start | bytes 393224 | tf_op jit(solution)/shard_map/ppermute | solution.py:441

commit v6 on v5

--- a/solution.py
+++ b/solution.py
@@ -113,7 +113,10 @@
     )
 
 
-def from_complex(a, b, c, d):
+def from_complex(a, b, c, d, with_first=True):
+    if not with_first:
+        top = jnp.concatenate([a + c, b + d], axis=1)
+        return jnp.concatenate([top, jnp.concatenate([b - d, c - a], axis=1)], axis=0)
     top = jnp.concatenate([fix_first(a[:8], a + c), fix_first(b[:8], b + d)], axis=1)
     low = jnp.concatenate([fix_first(c[:8], b - d), fix_first(d[:8], c - a)], axis=1)
     return jnp.concatenate([top, low], axis=0)
@@ -319,14 +322,23 @@
     store_spectrum(held, 0, to_complex(rows_forward(row_e, row_o, turned_ratio)))
 
     def filtered(k):
+        spectra = load_spectrum(held, 0)
+        half = spectra[0].shape[0]
+        step = half // 2
         planes = []
-        a, b, c, d = load_spectrum(held, 0)
         for i in range(2):
-            ha, hb, hc, hd = load_spectrum(spectrum, k + i)
-            plane = from_complex(a * ha + b * hb, b * ha - a * hb, c * hc + d * hd, d * hc - c * hd)
-            high, low = split(plane)
-            both = dot(high, col_i[...])
-            planes.append(both[:, :LANES] + (both[:, LANES:] + dot(low, col_i[:, :LANES])))
+            kernel = load_spectrum(spectrum, k + i)
+            pieces = []
+            for start in (0, step):
+                rows = slice(start, start + step)
+                a, b, c, d = (x[rows] for x in spectra)
+                ha, hb, hc, hd = (x[rows] for x in kernel)
+                parts = (a * ha + b * hb, b * ha - a * hb, c * hc + d * hd, d * hc - c * hd)
+                high, low = split(from_complex(*parts, start == 0))
+                both = dot(high, col_i[...])
+                pieces.append(both[:, :LANES] + (both[:, LANES:] + dot(low, col_i[:, :LANES])))
+            upper, lower = [p[:step] for p in pieces], [p[step:] for p in pieces]
+            planes.append(jnp.concatenate(upper + lower, axis=0))
         return jnp.concatenate(planes, axis=1)
 
     components = weights.shape[0]

time: 18.2 us -> 18.2 us (level)
  no operation moved by 1% of the time
where the time goes in v6:
time: 18.2 us; the launch traced here: 18 us
  Pallas kernels  11.6 us (64%)
  starting transfers between devices  5.08 us (28%)
  waiting for transfers between devices  1.27 us (7%)
    pallas_call x4, Pallas kernels, call(): pl.pallas_call(kernel, in_specs=[pl.BlockSpec(memory_space=space)] * len(...  11.6 us
    ppermute x1, starting transfers between devices, local(): lax.ppermute(packed_i, 'col', within)  4.32 us
    ppermute x1, waiting for transfers between devices, local(): lax.ppermute(packed_i, 'col', within)  0.91 us
    ppermute x1, starting transfers between devices, local(): received_o = lax.ppermute(edge_o, 'col', between)  0.68 us
  transfers between devices with their start and end apart: 3, of which 2 were waited for; matrix products, arithmetic and copies ran while one was open for 0% of the time, Pallas kernels for 23%

profile of v6, /device:TPU:0, one launch (start us, length us, event | category | flops | bytes accessed | tf_op | source)
XLA Modules:
  0.0 18.0 jit_solution(7981135628262972849)
XLA Ops:
  0.0 4.6 %outer_blur.1 = (f32[8,320,256]{2,1,0:T(8,128)S(1)}, f32[256,256]{1,0:T(8,128)S(1)}, f32[256,128]{1,0:T(8,128)S(1)}, bf16[160,480]{1,0:T(8,128)(2,1)S(1)}, bf16[...) custom-call(f32[129,8,129]{2,1,0:T(8,128)} %bitcast.1, ...), custom_call_target="tpu_custom_call" | custom-call | flops 30198988 | bytes 54886 | tf_op jit(solution)/shard_map/outer_blur/pallas_call | solution.py:381
  4.6 0.7 %collective-permute-start = (f32[256,256]{1,0:T(8,128)S(1)}, f32[256,256]{1,0:T(8,128)S(1)}, u32[]{:S(2)}, u32[]{:S(2)}) collective-permute-start(f32[256,256]{1,0:T(8,128)S(1)} %get-tuple-element.30.refs_8_), channel_id=1, source_target_pairs={{1,2},{3,4},{5,6},{7,8},{9,10},{11,12},{13,14},{2,1},{4,3},{6,5},{... | collective-permute-start | bytes 786440 | tf_op jit(solution)/shard_map/ppermute | solution.py:447
  5.3 0.0 copy-start
  5.3 0.0 copy-start.1
  5.3 0.0 copy-start.2
  5.3 1.9 %inner_blur.1 = (f32[256,128]{1,0:T(8,128)S(1)}, f32[256,128]{1,0:T(8,128)S(1)}, f32[256,128]{1,0:T(8,128)S(1)}) custom-call(f32[256,256]{1,0:T(8,128)S(1)} %get-tuple-element.23.est.refs_0_, f32[256,256]{1,0:T(8,128)S(1)} %get-tuple-element.24.obs.refs_1_, f32[256,256]{1,0:T(8,128)S(1)} %get-tuple-element.25.bg.refs_2_, ...), custom_call_target="tpu_custom_call" | custom-call | flops 15099494 | bytes 72335 | tf_op jit(solution)/shard_map/inner_blur/pallas_call | solution.py:381
  7.3 4.3 %collective-permute-start.2 = (f32[256,128]{1,0:T(8,128)S(1)}, f32[256,128]{1,0:T(8,128)S(1)}, u32[]{:S(2)}, u32[]{:S(2)}) collective-permute-start(f32[256,128]{1,0:T(8,128)S(1)} %get-tuple-element.40), channel_id=1, source_target_pairs={{0,1},{1,0},{2,3},{3,2},{4,5},{5,4},{6,7},{7,6},{8,9},{9,8},{10,11... | collective-permute-start | bytes 393224 | tf_op jit(solution)/shard_map/ppermute | solution.py:453
  11.6 0.1 collective-permute-start.1
  11.7 0.9 %collective-permute-done.2.refs_10_ = f32[256,128]{1,0:T(8,128)S(1)} collective-permute-done((f32[256,128]{1,0:T(8,128)S(1)}, f32[256,128]{1,0:T(8,128)S(1)}, u32[]{:S(2)}, u32[]{:S(2)}) %collective-permute-start.2) | collective-permute-done | bytes 131104 | tf_op jit(solution)/shard_map/ppermute | solution.py:453
  12.6 0.4 %collective-permute-done.1.refs_9_ = f32[256,128]{1,0:T(8,128)S(1)} collective-permute-done((f32[256,128]{1,0:T(8,128)S(1)}, f32[256,128]{1,0:T(8,128)S(1)}, u32[]{:S(2)}, u32[]{:S(2)}) %collective-permute-start.1) | collective-permute-done | bytes 131104 | tf_op jit(solution)/shard_map/ppermute | solution.py:453
  12.9 0.0 copy-done
  12.9 0.0 copy-done.1
  12.9 0.0 copy-done.2
  12.9 2.2 %inner_correct.1.refs_12_ = f32[256,128]{1,0:T(8,128)S(1)} custom-call(f32[256,256]{1,0:T(8,128)S(1)} %get-tuple-element.23.est.refs_0_, f32[256,256]{1,0:T(8,128)S(1)} %get-tuple-element.24.obs.refs_1_, f32[256,256]{1,0:T(8,128)S(1)} %get-tuple-element.25.bg.refs_2_, f32[256,256]{1,0:T(8,128)S(1)} %copy-done.1, ...), custom_call_target="tpu_custom_call" | custom-call | flops 15099494 | bytes 80855 | tf_op jit(solution)/shard_map/inner_correct/pallas_call | solution.py:381
  15.1 0.0 collective-permute-done.refs_9_
  15.1 2.9 %outer_correct.1 = f32[256,256]{1,0:T(8,128)} custom-call(f32[256,256]{1,0:T(8,128)S(1)} %get-tuple-element.23.est.refs_0_, f32[256,256]{1,0:T(8,128)S(1)} %get-tuple-element.24.obs.refs_1_, f32[256,256]{1,0:T(8,128)S(1)} %get-tuple-element.25.bg.refs_2_, f32[256,256]{1,0:T(8,128)S(1)} %copy-done.1, s32[256,256]{1,0:T(8,128)S(1)} %get-tuple-element.26.valid.refs_4_, ...), custom_call_target="tpu_custom_call" | custom-call | flops 15099494 | bytes 83476 | tf_op jit(solution)/shard_map/outer_correct/pallas_call | solution.py:381
Async XLA Ops:
  4.6 10.6 %collective-permute-start = (f32[256,256]{1,0:T(8,128)S(1)}, f32[256,256]{1,0:T(8,128)S(1)}, u32[]{:S(2)}, u32[]{:S(2)}) collective-permute-start(f32[256,256]{1,0:T(8,128)S(1)} %get-tuple-element.30.refs_8_), channel_id=1, source_target_pairs={{1,2},{3,4},{5,6},{7,8},{9,10},{11,12},{13,14},{2,1},{4,3},{6,5},{... | collective-permute-start | bytes 786440 | tf_op jit(solution)/shard_map/ppermute | solution.py:447
  5.3 7.7 %copy-start = (bf16[768,256]{1,0:T(8,128)(2,1)S(1)}, bf16[768,256]{1,0:T(8,128)(2,1)}, u32[]{:S(2)}) copy-start(bf16[768,256]{1,0:T(8,128)(2,1)} %constant.30.clone.refs_15_) | copy-start | bytes 1179652
  5.3 7.7 %copy-start.1 = (f32[256,256]{1,0:T(8,128)S(1)}, f32[256,256]{1,0:T(8,128)}, u32[]{:S(2)}) copy-start(f32[256,256]{1,0:T(8,128)} %refs_3_.4) | copy-start | bytes 786436
  5.3 7.6 %copy-start.2 = (bf16[256,256]{1,0:T(8,128)(2,1)S(1)}, bf16[256,256]{1,0:T(8,128)(2,1)}, u32[]{:S(2)}) copy-start(bf16[256,256]{1,0:T(8,128)(2,1)} %constant.32.clone.refs_18_) | copy-start | bytes 393220
  7.3 5.3 %collective-permute-start.2 = (f32[256,128]{1,0:T(8,128)S(1)}, f32[256,128]{1,0:T(8,128)S(1)}, u32[]{:S(2)}, u32[]{:S(2)}) collective-permute-start(f32[256,128]{1,0:T(8,128)S(1)} %get-tuple-element.40), channel_id=1, source_target_pairs={{0,1},{1,0},{2,3},{3,2},{4,5},{5,4},{6,7},{7,6},{8,9},{9,8},{10,11... | collective-permute-start | bytes 393224 | tf_op jit(solution)/shard_map/ppermute | solution.py:453
  11.6 1.3 %collective-permute-start.1 = (f32[256,128]{1,0:T(8,128)S(1)}, f32[256,128]{1,0:T(8,128)S(1)}, u32[]{:S(2)}, u32[]{:S(2)}) collective-permute-start(f32[256,128]{1,0:T(8,128)S(1)} %get-tuple-element.39.refs_8_), channel_id=1, source_target_pairs={{0,1},{1,0},{2,3},{3,2},{4,5},{5,4},{6,7},{7,6},{8,9},{9,8},{10,11... | collective-permute-start | bytes 393224 | tf_op jit(solution)/shard_map/ppermute | solution.py:453
